TPU v7x, 32 devices: a whole 2x2x4 slice. The times are simulated.
32 devices in a mesh: dp: 4 (over z), wide: 4 (over x, core), narrow: 2 (over y).
Axes of the slice: x: 2, y: 2, z: 4, core: 2. Of those that a mesh axis runs over, the one named last changes fastest.
Arguments:
- tokens: bfloat16 [16384, 768], P(('dp', 'wide')), may hold values from -6 to 6
- memory: bfloat16 [32, 2048, 768], P(('dp', 'wide')), may hold values from -6 to 6
- cotangent: bfloat16 [16384, 768], P(('dp', 'wide')), may hold values from -6 to 6
- norm1_gain: bfloat16 [768], P('wide'), may hold values from 0.5 to 1.5
- norm2_gain: bfloat16 [768], P('wide'), may hold values from 0.5 to 1.5
- norm3_gain: bfloat16 [768], P('wide'), may hold values from 0.5 to 1.5
- q_weight: bfloat16 [768, 768], P('wide', 'narrow'), may hold values from -0.3125 to 0.3125
- k_weight: bfloat16 [768, 768], P('wide', 'narrow'), may hold values from -0.3125 to 0.3125
- v_weight: bfloat16 [768, 768], P('wide', 'narrow'), may hold values from -0.21875 to 0.21875
- o_weight: bfloat16 [768, 768], P('wide', 'narrow'), may hold values from -0.4375 to 0.4375
- cross_q: bfloat16 [768, 768], P('wide', 'narrow'), may hold values from -0.3125 to 0.3125
- cross_k: bfloat16 [768, 768], P('wide', 'narrow'), may hold values from -0.3125 to 0.3125
- cross_v: bfloat16 [768, 768], P('wide', 'narrow'), may hold values from -0.21875 to 0.21875
- cross_o: bfloat16 [768, 768], P('wide', 'narrow'), may hold values from -1.25 to 1.25
- gate_weight: bfloat16 [768, 2048], P('wide', 'narrow'), may hold values from -0.21875 to 0.21875
- up_weight: bfloat16 [768, 2048], P('wide', 'narrow'), may hold values from -0.21875 to 0.21875
- down_weight: bfloat16 [768, 2048], P('wide', 'narrow'), may hold values from -0.1875 to 0.1875
- segment_ids: int32 [16, 1024], P(('dp', 'wide')), may hold values from 0 to 7, never falling along the last dimension, each value on 1 to 256 neighbouring positions
- block_ids: int32 [16, 1024], P(('dp', 'wide')), may hold values from 0 to 63, never falling along the last dimension, each value on 1 to 32 neighbouring positions
- image_table: int32 [16, 8], P(('dp', 'wide')), may hold values from 0 to 1
Outputs:
- output: bfloat16 [16384, 768], P(('dp', 'wide'))
- tokens_grad: bfloat16 [16384, 768], P(('dp', 'wide'))
- memory_grad: bfloat16 [32, 2048, 768], P(('dp', 'wide'), None, 'narrow')
- norm1_gain_grad: float32 [768], P('wide')
- norm2_gain_grad: float32 [768], P('wide')
- norm3_gain_grad: float32 [768], P('wide')
- q_weight_grad: float32 [768, 768], P('wide', 'narrow')
- k_weight_grad: float32 [768, 768], P('wide', 'narrow')
- v_weight_grad: float32 [768, 768], P('wide', 'narrow')
- o_weight_grad: float32 [768, 768], P('wide', 'narrow')
- cross_q_grad: float32 [768, 768], P('wide', 'narrow')
- cross_k_grad: float32 [768, 768], P('wide', 'narrow')
- cross_v_grad: float32 [768, 768], P('wide', 'narrow')
- cross_o_grad: float32 [768, 768], P('wide', 'narrow')
- gate_weight_grad: float32 [768, 2048], P('wide', 'narrow')
- up_weight_grad: float32 [768, 2048], P('wide', 'narrow')
- down_weight_grad: float32 [768, 2048], P('wide', 'narrow')
Inputs may be any that keep to these rules, and one draw needn't show every extreme that they name: `segment_ids`: in each decoder row the ids never fall and every id occurs, each on 1 to 256 positions, some id on exactly that many. `block_ids`: in each decoder row the ids never fall and every id occurs, each on 1 to 32 positions, some id on exactly that many. `image_table`: entry r, s names one of the 2 images stored with decoder row r, the images r * 2 to r * 2 + 1.
All inputs are finite; a program needn't handle non-finite values.
Results may differ from a plain program's by a relative error of at most 0.038.
Values may be sent and summed in bfloat16 or wider, within the bound.
No kernel may reach another device: no remote copies, remote signals or barrier semaphores. Data moves between devices by JAX's collectives and lax.ppermute only.
A program may use at most 384 MiB of HBM per device.

v0:
```python
import jax
import jax.numpy as jnp
from jax import lax
from jax.sharding import PartitionSpec as P

HEAD_DIM = 64


EPSILON = 1e-06
ROOT_TWO_OVER_PI = 0.7978845608028654


def rms_norm(values, gain_vector):
    factor = lax.rsqrt(jnp.mean(values * values, axis=1, keepdims=True) + EPSILON)
    return values * factor * gain_vector[None, :]


def gelu_tanh(values):
    return (
        0.5
        * values
        * (1.0 + jnp.tanh(ROOT_TWO_OVER_PI * (values + 0.044715 * values * values * values)))
    )


def gated_units(gate_value, up_value):
    return gelu_tanh(gate_value) * up_value


def product(left, right):
    return jnp.dot(left, right, preferred_element_type=jnp.float32)


def contract_rows(left, right):
    return lax.dot_general(
        left, right, (((0,), (0,)), ((), ())), preferred_element_type=jnp.float32
    )


def contract_cols(left, right):
    return lax.dot_general(
        left, right, (((1,), (1,)), ((), ())), preferred_element_type=jnp.float32
    )


def sum_branch(partial_sum):
    return lax.psum_scatter(
        partial_sum.astype(jnp.bfloat16), "narrow", scatter_dimension=0, tiled=True
    ).astype(jnp.float32)


def sum_inputs(partial_sum):
    return lax.psum_scatter(
        partial_sum.astype(jnp.bfloat16), "narrow", scatter_dimension=0, tiled=True
    ).astype(jnp.float32)


def whole_rows(share):
    return lax.all_gather(share, "narrow", axis=0, tiled=True)


def whole_grads(share):
    return lax.all_gather(share, "narrow", axis=0, tiled=True)


def norm_backward(values, gain_vector, upstream):
    unused, pullback = jax.vjp(rms_norm, values, gain_vector)
    return pullback(upstream)


def split_heads(matrix):
    return matrix.reshape(matrix.shape[0], matrix.shape[1] // HEAD_DIM, HEAD_DIM)


def attend_forward(queries, keys_all, values_all, visible_fn):
    total_rows = queries.shape[0]
    block_rows = min(512, total_rows)
    num_blocks = total_rows // block_rows
    head_count = queries.shape[1] // HEAD_DIM
    score_scale = HEAD_DIM ** (-0.5)
    key_heads = split_heads(keys_all)
    value_heads = split_heads(values_all)

    def one_block(inputs):
        query_part, offset = inputs
        visible = visible_fn(offset, block_rows)
        scores = (
            jnp.einsum("qhd,khd->hqk", query_part, key_heads, preferred_element_type=jnp.float32)
            * score_scale
        )
        scores = jnp.where(visible[None, :, :], scores, -jnp.inf)
        highest = jnp.max(scores, axis=2, keepdims=True)
        exponent = jnp.exp(scores - highest)
        normalizer = jnp.sum(exponent, axis=2, keepdims=True)
        probabilities = (exponent / normalizer).astype(jnp.bfloat16)
        mixed_rows = jnp.einsum(
            "hqk,khd->qhd", probabilities, value_heads, preferred_element_type=jnp.float32
        )
        return (mixed_rows.astype(jnp.bfloat16), (highest + jnp.log(normalizer))[:, :, 0])

    offsets = jnp.arange(num_blocks, dtype=jnp.int32) * block_rows
    mixed_rows, log_totals = lax.map(
        one_block, (queries.reshape(num_blocks, block_rows, head_count, HEAD_DIM), offsets)
    )
    return (mixed_rows.reshape(total_rows, head_count * HEAD_DIM), log_totals)


def attend_backward(queries, keys_all, values_all, grad_mixed, log_totals, visible_fn):
    total_rows = queries.shape[0]
    block_rows = min(512, total_rows)
    num_blocks = total_rows // block_rows
    head_count = queries.shape[1] // HEAD_DIM
    score_scale = HEAD_DIM ** (-0.5)
    key_heads = split_heads(keys_all)
    value_heads = split_heads(values_all)

    def one_block(running, inputs):
        key_grad, value_grad = running
        query_part, grad_part, log_part, offset = inputs
        visible = visible_fn(offset, block_rows)
        scores = (
            jnp.einsum("qhd,khd->hqk", query_part, key_heads, preferred_element_type=jnp.float32)
            * score_scale
        )
        scores = jnp.where(visible[None, :, :], scores, -jnp.inf)
        probabilities = jnp.exp(scores - log_part[:, :, None])
        low_probabilities = probabilities.astype(jnp.bfloat16)
        value_grad = value_grad + jnp.einsum(
            "hqk,qhd->khd", low_probabilities, grad_part, preferred_element_type=jnp.float32
        )
        prob_grad = jnp.einsum(
            "qhd,khd->hqk", grad_part, value_heads, preferred_element_type=jnp.float32
        )
        centre = jnp.sum(probabilities * prob_grad, axis=2, keepdims=True)
        score_grad = (probabilities * (prob_grad - centre)).astype(jnp.bfloat16)
        query_grad = (
            jnp.einsum("hqk,khd->qhd", score_grad, key_heads, preferred_element_type=jnp.float32)
            * score_scale
        )
        key_grad = (
            key_grad
            + jnp.einsum("hqk,qhd->khd", score_grad, query_part, preferred_element_type=jnp.float32)
            * score_scale
        )
        return ((key_grad, value_grad), query_grad)

    offsets = jnp.arange(num_blocks, dtype=jnp.int32) * block_rows
    zero_heads = jnp.zeros(key_heads.shape, jnp.float32)
    block_shape = (num_blocks, block_rows, head_count, HEAD_DIM)
    (key_grad, value_grad), query_grad = lax.scan(
        one_block,
        (zero_heads, zero_heads),
        (queries.reshape(block_shape), grad_mixed.reshape(block_shape), log_totals, offsets),
    )
    return (
        query_grad.reshape(total_rows, -1).astype(jnp.bfloat16),
        key_grad.reshape(keys_all.shape[0], -1).astype(jnp.bfloat16),
        value_grad.reshape(values_all.shape[0], -1).astype(jnp.bfloat16),
    )


def reorder_rows(gradient, wide_size, data_size):
    trailing = gradient.shape[1:]
    split_rows = gradient.reshape(
        (wide_size, data_size, gradient.shape[0] // (wide_size * data_size)) + trailing
    )
    return jnp.swapaxes(split_rows, 0, 1).reshape(gradient.shape)


def local(
    tokens,
    memory,
    cotangent,
    norm1_gain,
    norm2_gain,
    norm3_gain,
    q_weight,
    k_weight,
    v_weight,
    o_weight,
    cross_q,
    cross_k,
    cross_v,
    cross_o,
    gate_weight,
    up_weight,
    down_weight,
    segment_ids,
    block_ids,
    image_table,
):
    gathered = (
        lax.all_gather(norm1_gain, "wide", axis=0, tiled=True),
        lax.all_gather(norm2_gain, "wide", axis=0, tiled=True),
        lax.all_gather(norm3_gain, "wide", axis=0, tiled=True),
        lax.all_gather(q_weight, "wide", axis=0, tiled=True),
        lax.all_gather(k_weight, "wide", axis=0, tiled=True),
        lax.all_gather(v_weight, "wide", axis=0, tiled=True),
        lax.all_gather(o_weight, "wide", axis=0, tiled=True),
        lax.all_gather(cross_q, "wide", axis=0, tiled=True),
        lax.all_gather(cross_k, "wide", axis=0, tiled=True),
        lax.all_gather(cross_v, "wide", axis=0, tiled=True),
        lax.all_gather(cross_o, "wide", axis=0, tiled=True),
        lax.all_gather(gate_weight, "wide", axis=0, tiled=True),
        lax.all_gather(up_weight, "wide", axis=0, tiled=True),
        lax.all_gather(down_weight, "wide", axis=0, tiled=True),
    )
    first_gain = gathered[0].astype(jnp.float32)
    second_gain = gathered[1].astype(jnp.float32)
    third_gain = gathered[2].astype(jnp.float32)
    query_weight = gathered[3]
    key_weight = gathered[4]
    value_weight = gathered[5]
    out_weight = gathered[6]
    cross_query_weight = gathered[7]
    cross_key_weight = gathered[8]
    cross_value_weight = gathered[9]
    cross_out_weight = gathered[10]
    gate_matrix = gathered[11]
    up_matrix = gathered[12]
    down_matrix = gathered[13]
    share_rows = tokens.shape[0] // lax.axis_size("narrow")
    share_start = lax.axis_index("narrow") * share_rows
    segments = segment_ids.reshape(-1)
    blocks = block_ids.reshape(-1)
    segment_count = image_table.shape[1]
    table_row = image_table.reshape(-1)
    token_images = jnp.sum(
        jnp.where(
            segments[:, None] == jnp.arange(segment_count, dtype=jnp.int32)[None, :],
            table_row[None, :],
            0,
        ),
        axis=1,
    )
    flat_memory = memory.reshape(-1, memory.shape[2])
    key_images = jnp.arange(flat_memory.shape[0], dtype=jnp.int32) // memory.shape[1]

    def self_visible(offset, count_rows):
        query_segments = lax.dynamic_slice_in_dim(segments, offset, count_rows)
        query_blocks = lax.dynamic_slice_in_dim(blocks, offset, count_rows)
        return (query_segments[:, None] == segments[None, :]) & (
            blocks[None, :] <= query_blocks[:, None]
        )

    def cross_visible(offset, count_rows):
        query_images = lax.dynamic_slice_in_dim(token_images, offset, count_rows)
        return query_images[:, None] == key_images[None, :]

    stream = tokens.astype(jnp.float32)
    stream_share = lax.dynamic_slice_in_dim(stream, share_start, share_rows, 0)
    normed_one = rms_norm(stream, first_gain).astype(jnp.bfloat16)
    queries = product(normed_one, query_weight).astype(jnp.bfloat16)
    keys_self = product(normed_one, key_weight).astype(jnp.bfloat16)
    values_self = product(normed_one, value_weight).astype(jnp.bfloat16)
    attended, self_log_totals = attend_forward(queries, keys_self, values_self, self_visible)
    middle = stream_share + sum_branch(contract_cols(attended, out_weight))
    normed_two = whole_rows(rms_norm(middle, second_gain).astype(jnp.bfloat16))
    cross_queries = product(normed_two, cross_query_weight).astype(jnp.bfloat16)
    cross_keys = product(flat_memory, cross_key_weight).astype(jnp.bfloat16)
    cross_values = product(flat_memory, cross_value_weight).astype(jnp.bfloat16)
    crossed, cross_log_totals = attend_forward(
        cross_queries, cross_keys, cross_values, cross_visible
    )
    after_cross = middle + sum_branch(contract_cols(crossed, cross_out_weight))
    normed_three = whole_rows(rms_norm(after_cross, third_gain).astype(jnp.bfloat16))
    gate_value = product(normed_three, gate_matrix)
    up_value = product(normed_three, up_matrix)
    hidden = gated_units(gate_value, up_value).astype(jnp.bfloat16)
    output = whole_rows(
        (after_cross + sum_branch(contract_cols(hidden, down_matrix))).astype(jnp.bfloat16)
    )
    grad_share = lax.dynamic_slice_in_dim(cotangent, share_start, share_rows, 0).astype(jnp.float32)
    down_grad = contract_rows(cotangent, hidden)
    grad_hidden = product(cotangent, down_matrix)
    unused, gated_pullback = jax.vjp(gated_units, gate_value, up_value)
    grad_gate, grad_up = gated_pullback(grad_hidden)
    grad_gate = grad_gate.astype(jnp.bfloat16)
    grad_up = grad_up.astype(jnp.bfloat16)
    gate_grad = contract_rows(normed_three, grad_gate)
    up_grad = contract_rows(normed_three, grad_up)
    grad_normed = sum_inputs(
        contract_cols(grad_gate, gate_matrix) + contract_cols(grad_up, up_matrix)
    )
    norm_part, third_share_grad = norm_backward(after_cross, third_gain, grad_normed)
    grad_after = grad_share + norm_part
    low_after = whole_grads(grad_after.astype(jnp.bfloat16))
    cross_out_grad = contract_rows(low_after, crossed)
    grad_crossed = product(low_after, cross_out_weight).astype(jnp.bfloat16)
    grad_cross_queries, grad_cross_keys, grad_cross_values = attend_backward(
        cross_queries, cross_keys, cross_values, grad_crossed, cross_log_totals, cross_visible
    )
    cross_query_grad = contract_rows(normed_two, grad_cross_queries)
    cross_key_grad = contract_rows(flat_memory, grad_cross_keys)
    cross_value_grad = contract_rows(flat_memory, grad_cross_values)
    memory_part = contract_cols(grad_cross_keys, cross_key_weight) + contract_cols(
        grad_cross_values, cross_value_weight
    )
    memory_shard = lax.psum_scatter(
        memory_part.astype(jnp.bfloat16), "narrow", scatter_dimension=1, tiled=True
    )
    memory_grad = memory_shard.reshape(memory.shape[0], memory.shape[1], -1)
    grad_normed = sum_inputs(contract_cols(grad_cross_queries, cross_query_weight))
    norm_part, second_share_grad = norm_backward(middle, second_gain, grad_normed)
    grad_middle = grad_after + norm_part
    low_middle = whole_grads(grad_middle.astype(jnp.bfloat16))
    out_grad = contract_rows(low_middle, attended)
    grad_attended = product(low_middle, out_weight).astype(jnp.bfloat16)
    grad_queries, grad_keys, grad_values = attend_backward(
        queries, keys_self, values_self, grad_attended, self_log_totals, self_visible
    )
    query_grad = contract_rows(normed_one, grad_queries)
    key_grad = contract_rows(normed_one, grad_keys)
    value_grad = contract_rows(normed_one, grad_values)
    grad_normed = sum_inputs(
        contract_cols(grad_queries, query_weight)
        + contract_cols(grad_keys, key_weight)
        + contract_cols(grad_values, value_weight)
    )
    norm_part, first_share_grad = norm_backward(stream_share, first_gain, grad_normed)
    tokens_grad = whole_grads((grad_middle + norm_part).astype(jnp.bfloat16))
    gain_totals = lax.psum((first_share_grad, second_share_grad, third_share_grad), "narrow")
    first_gain_grad = gain_totals[0]
    second_gain_grad = gain_totals[1]
    third_gain_grad = gain_totals[2]
    wide_size = lax.axis_size("wide")
    data_size = lax.axis_size("dp")
    listing = [
        first_gain_grad,
        second_gain_grad,
        third_gain_grad,
        query_grad,
        key_grad,
        value_grad,
        out_grad,
        cross_query_grad,
        cross_key_grad,
        cross_value_grad,
        cross_out_grad,
        gate_grad,
        up_grad,
        down_grad,
    ]
    ordered = [reorder_rows(gradient, wide_size, data_size) for gradient in listing]
    pieces = (
        lax.psum_scatter(ordered[0], ("dp", "wide"), scatter_dimension=0, tiled=True),
        lax.psum_scatter(ordered[1], ("dp", "wide"), scatter_dimension=0, tiled=True),
        lax.psum_scatter(ordered[2], ("dp", "wide"), scatter_dimension=0, tiled=True),
        lax.psum_scatter(ordered[3], ("dp", "wide"), scatter_dimension=0, tiled=True),
        lax.psum_scatter(ordered[4], ("dp", "wide"), scatter_dimension=0, tiled=True),
        lax.psum_scatter(ordered[5], ("dp", "wide"), scatter_dimension=0, tiled=True),
        lax.psum_scatter(ordered[6], ("dp", "wide"), scatter_dimension=0, tiled=True),
        lax.psum_scatter(ordered[7], ("dp", "wide"), scatter_dimension=0, tiled=True),
        lax.psum_scatter(ordered[8], ("dp", "wide"), scatter_dimension=0, tiled=True),
        lax.psum_scatter(ordered[9], ("dp", "wide"), scatter_dimension=0, tiled=True),
        lax.psum_scatter(ordered[10], ("dp", "wide"), scatter_dimension=0, tiled=True),
        lax.psum_scatter(ordered[11], ("dp", "wide"), scatter_dimension=0, tiled=True),
        lax.psum_scatter(ordered[12], ("dp", "wide"), scatter_dimension=0, tiled=True),
        lax.psum_scatter(ordered[13], ("dp", "wide"), scatter_dimension=0, tiled=True),
    )
    totals = (
        lax.all_gather(pieces[0].astype(jnp.bfloat16), "dp", axis=0, tiled=True).astype(
            jnp.float32
        ),
        lax.all_gather(pieces[1].astype(jnp.bfloat16), "dp", axis=0, tiled=True).astype(
            jnp.float32
        ),
        lax.all_gather(pieces[2].astype(jnp.bfloat16), "dp", axis=0, tiled=True).astype(
            jnp.float32
        ),
        lax.all_gather(pieces[3].astype(jnp.bfloat16), "dp", axis=0, tiled=True).astype(
            jnp.float32
        ),
        lax.all_gather(pieces[4].astype(jnp.bfloat16), "dp", axis=0, tiled=True).astype(
            jnp.float32
        ),
        lax.all_gather(pieces[5].astype(jnp.bfloat16), "dp", axis=0, tiled=True).astype(
            jnp.float32
        ),
        lax.all_gather(pieces[6].astype(jnp.bfloat16), "dp", axis=0, tiled=True).astype(
            jnp.float32
        ),
        lax.all_gather(pieces[7].astype(jnp.bfloat16), "dp", axis=0, tiled=True).astype(
            jnp.float32
        ),
        lax.all_gather(pieces[8].astype(jnp.bfloat16), "dp", axis=0, tiled=True).astype(
            jnp.float32
        ),
        lax.all_gather(pieces[9].astype(jnp.bfloat16), "dp", axis=0, tiled=True).astype(
            jnp.float32
        ),
        lax.all_gather(pieces[10].astype(jnp.bfloat16), "dp", axis=0, tiled=True).astype(
            jnp.float32
        ),
        lax.all_gather(pieces[11].astype(jnp.bfloat16), "dp", axis=0, tiled=True).astype(
            jnp.float32
        ),
        lax.all_gather(pieces[12].astype(jnp.bfloat16), "dp", axis=0, tiled=True).astype(
            jnp.float32
        ),
        lax.all_gather(pieces[13].astype(jnp.bfloat16), "dp", axis=0, tiled=True).astype(
            jnp.float32
        ),
    )
    return (
        output,
        tokens_grad,
        memory_grad,
        totals[0],
        totals[1],
        totals[2],
        totals[3],
        totals[4],
        totals[5],
        totals[6],
        totals[7],
        totals[8],
        totals[9],
        totals[10],
        totals[11],
        totals[12],
        totals[13],
    )


def solution(mesh):
    in_specs = (
        P(("dp", "wide"), None),
        P(("dp", "wide"), None, None),
        P(("dp", "wide"), None),
        P("wide"),
        P("wide"),
        P("wide"),
        P("wide", "narrow"),
        P("wide", "narrow"),
        P("wide", "narrow"),
        P("wide", "narrow"),
        P("wide", "narrow"),
        P("wide", "narrow"),
        P("wide", "narrow"),
        P("wide", "narrow"),
        P("wide", "narrow"),
        P("wide", "narrow"),
        P("wide", "narrow"),
        P(("dp", "wide"), None),
        P(("dp", "wide"), None),
        P(("dp", "wide"), None),
    )
    out_specs = (
        P(("dp", "wide"), None),
        P(("dp", "wide"), None),
        P(("dp", "wide"), None, "narrow"),
        P("wide"),
        P("wide"),
        P("wide"),
        P("wide", "narrow"),
        P("wide", "narrow"),
        P("wide", "narrow"),
        P("wide", "narrow"),
        P("wide", "narrow"),
        P("wide", "narrow"),
        P("wide", "narrow"),
        P("wide", "narrow"),
        P("wide", "narrow"),
        P("wide", "narrow"),
        P("wide", "narrow"),
    )
    return jax.shard_map(local, mesh=mesh, in_specs=in_specs, out_specs=out_specs, check_vma=False)
```

profile of v0, /device:TPU:0, one launch (start us, length us, event | category | flops | bytes accessed | tf_op | source)
XLA Modules:
  0.0 1786.5 jit_solution(14859002636926100726)
XLA Ops:
  58.3 27.0 %while.55 = (s32[]{:T(128)}, bf16[2,512,6,64]{1,3,2,0:T(8,128)(2,1)S(1)}, f32[2,6,512]{2,1,0:T(8,128)S(1)}, s32[2]{0:T(128)S(1)}, s32[1024]{0:T(1024)S(1)}, /*in...) while((s32[]{:T(128)}, ...), condition=%wide.region_4.5_spmd, body=%wide.region_1.4_spmd.sunk | while | flops 844821504 | bytes 42344652 | solution.py:102
  153.2 141.2 %while.56 = (s32[]{:T(128)}, bf16[2,512,6,64]{1,3,2,0:T(8,128)(2,1)}, f32[2,6,512]{2,1,0:T(8,128)S(1)}, s32[2]{0:T(128)S(1)}, s32[1024]{0:T(1024)S(1)}, /*index=...) while((s32[]{:T(128)}, ...), condition=%wide.region_11.12_spmd.clone, body=%wide.region_8.11_spmd.clone.sunk | while | flops 3374543872 | bytes 166611120 | solution.py:102
  157.6 22.1 %fusion.236 = (f32[6,512]{1,0:T(8,128)S(1)}, f32[6,512,4096]{2,1,0:T(8,128)}) fusion(pred[512,4096]{1,0:T(8,128)(4,1)S(1)} %broadcast_compare_fusion.4, bf16[4096,6,64]{0,2,1:T(8,128)(2,1)} %get-tuple-element.1069, bf16[2,512,6,64]{1,3,2,0:T(8,128)(2,1)S(1)} %get-tuple-element.1068, s32[]{:T(128)S(6)} %copy.250), kind=kOutput, calls=%fused_computation.22.clone.1 | convolution fusion | flops 1648358400 | bytes 55980036 | tf_op jit(solution)/shard_map/while/body/eval_jaxpr/qhd,khd->hqk/dot_general | solution.py:88
  179.6 22.6 %fusion.237 = f32[6,512]{1,0:T(8,128)S(1)} fusion(f32[6,512,4096]{2,1,0:T(8,128)} %get-tuple-element.968, f32[6,512]{1,0:T(8,128)S(1)} %get-tuple-element.969, pred[512,4096]{1,0:T(8,128)(4,1)S(1)} %broadcast_compare_fusion.4), kind=kLoop, calls=%fused_computation.23.clone.1 | loop fusion | flops 50328576 | bytes 52453376 | tf_op jit(solution)/shard_map/while/body/eval_jaxpr/reduce_sum | solution.py:94
  227.9 22.1 %fusion.236 = (f32[6,512]{1,0:T(8,128)S(1)}, f32[6,512,4096]{2,1,0:T(8,128)}) fusion(pred[512,4096]{1,0:T(8,128)(4,1)S(1)} %broadcast_compare_fusion.4, bf16[4096,6,64]{0,2,1:T(8,128)(2,1)} %get-tuple-element.1069, bf16[2,512,6,64]{1,3,2,0:T(8,128)(2,1)S(1)} %get-tuple-element.1068, s32[]{:T(128)S(6)} %copy.250), kind=kOutput, calls=%fused_computation.22.clone.1 | convolution fusion | flops 1648358400 | bytes 55980036 | tf_op jit(solution)/shard_map/while/body/eval_jaxpr/qhd,khd->hqk/dot_general | solution.py:88
  250.0 22.6 %fusion.237 = f32[6,512]{1,0:T(8,128)S(1)} fusion(f32[6,512,4096]{2,1,0:T(8,128)} %get-tuple-element.968, f32[6,512]{1,0:T(8,128)S(1)} %get-tuple-element.969, pred[512,4096]{1,0:T(8,128)(4,1)S(1)} %broadcast_compare_fusion.4), kind=kLoop, calls=%fused_computation.23.clone.1 | loop fusion | flops 50328576 | bytes 52453376 | tf_op jit(solution)/shard_map/while/body/eval_jaxpr/reduce_sum | solution.py:94
  272.5 21.7 %fusion.238 = bf16[2,512,6,64]{1,3,2,0:T(8,128)(2,1)} fusion(bf16[2,512,6,64]{1,3,2,0:T(8,128)(2,1)} %get-tuple-element.1053, s32[]{:T(128)S(6)} %copy.250, bf16[4096,6,64]{0,2,1:T(8,128)(2,1)} %get-tuple-element.1070, f32[6,512,4096]{2,1,0:T(8,128)} %get-tuple-element.968, f32[6,512]{1,0:T(8,128)S(1)} %fusion.237, ...), kind=kOutput, calls=%fused_computation.28.clone.1 | convolution fusion | flops 1673723904 | bytes 55992324 | tf_op jit(solution)/shard_map/while/body/eval_jaxpr/hqk,khd->qhd/dot_general | solution.py:96
  300.4 25.6 %reduce-scatter.23.cloned.1.call-done = bf16[512,768]{1,0:T(8,128)(2,1)} async-done(((bf16[1024,768]{1,0:T(8,128)(2,1)}), bf16[512,768]{1,0:T(8,128)(2,1)}) %reduce-scatter.23.cloned.1.call-update) | async-done | bytes 786448 | tf_op jit(solution)/shard_map/reduce_scatter | solution.py:47
  331.1 25.8 %all-gather.12.cloned.1.call-done = bf16[1024,768]{1,0:T(8,128)(2,1)} async-done(((bf16[512,768]{1,0:T(8,128)(2,1)}), bf16[1024,768]{1,0:T(8,128)(2,1)}) %all-gather.12.cloned.1.call-update) | async-done | bytes 1572880 | tf_op jit(solution)/shard_map/all_gather | solution.py:59
  414.9 26.2 %reduce-scatter.27.cloned.1.call-done = bf16[512,768]{1,0:T(8,128)(2,1)} async-done(((bf16[1024,768]{1,0:T(8,128)(2,1)}), bf16[512,768]{1,0:T(8,128)(2,1)}) %reduce-scatter.27.cloned.1.call-update) | async-done | bytes 786448 | tf_op jit(solution)/shard_map/reduce_scatter | solution.py:53
  446.7 27.1 %all-gather.22.cloned.1.call-done = bf16[1024,768]{1,0:T(8,128)(2,1)} async-done(((bf16[512,768]{1,0:T(8,128)(2,1)}), bf16[1024,768]{1,0:T(8,128)(2,1)}) %all-gather.22.cloned.1.call-update) | async-done | bytes 1572880 | tf_op jit(solution)/shard_map/all_gather | solution.py:63
  479.0 316.4 %while.57 = (s32[]{:T(128)}, f32[4096,6,64]{0,2,1:T(8,128)}, f32[4096,6,64]{0,2,1:T(8,128)}, bf16[2,512,6,64]{1,3,2,0:T(8,128)(2,1)}, bf16[2,512,6,64]{1,3,2,0:T...) while((s32[]{:T(128)}, f32[4096,6,64]{0,2,1:T(8,128)}, ...), condition=%wide.region_19.20_spmd.clone, body=%wide.region_17.19_spmd.clone.sunk | while | flops 8251995136 | bytes 422963392 | solution.py:150
  504.5 23.8 %bitcast_add_fusion.9 = f32[4096,6,64]{0,2,1:T(8,128)} fusion(f32[4096,6,64]{0,2,1:T(8,128)} %get-tuple-element.1090, f32[6,512,4096]{2,1,0:T(8,128)} %fusion.248, f32[6,512]{1,0:T(8,128)S(1)} %dynamic-slice_bitcast_fusion.4, pred[512,4096]{1,0:T(8,128)(4,1)S(1)} %broadcast_compare_fusion.5, pred[]{:T(512)S(6)} %compare.8, ...), kind=kOutput, calls=%fused_computation.49.clone.1 | convolution fusion | flops 1664090112 | bytes 65417220 | tf_op jit(solution)/shard_map/while/body/eval_jaxpr/hqk,qhd->khd/dot_general | solution.py:128
  528.3 37.2 %multiply_reduce_fusion.8 = (f32[6,512]{1,0:T(8,128)S(1)}, f32[6,512,4096]{2,1,0:T(8,128)}) fusion(f32[6,512,4096]{2,1,0:T(8,128)} %fusion.248, f32[6,512]{1,0:T(8,128)S(1)} %dynamic-slice_bitcast_fusion.4, pred[512,4096]{1,0:T(8,128)(4,1)S(1)} %broadcast_compare_fusion.5, bf16[4096,6,64]{0,2,1:T(8,128)(2,1)} %get-tuple-element.1112, ...), kind=kOutput, calls=%fused_computation.44.clone.1 | convolution fusion | flops 1673524224 | bytes 106323968 | tf_op jit(solution)/shard_map/while/body/eval_jaxpr/qhd,khd->hqk/dot_general | solution.py:131
  565.5 41.0 %multiply_convert_fusion.12 = bf16[6,512,4096]{2,1,0:T(8,128)(2,1)} fusion(f32[6,512,4096]{2,1,0:T(8,128)} %get-tuple-element.981, f32[6,512,4096]{2,1,0:T(8,128)} %fusion.248, f32[6,512]{1,0:T(8,128)S(1)} %get-tuple-element.982, f32[6,512]{1,0:T(8,128)S(1)} %dynamic-slice_bitcast_fusion.4, pred[512,4096]{1,0:T(8,128)(4,1)S(1)} %broadcast_compare_fusion.5), kind=kLoop, calls=%fused_computation.43.clone.1 | loop fusion | flops 75497472 | bytes 127950848 | tf_op jit(solution)/shard_map/while/body/eval_jaxpr/convert_element_type | solution.py:135
  661.0 25.0 %bitcast_add_fusion.9 = f32[4096,6,64]{0,2,1:T(8,128)} fusion(f32[4096,6,64]{0,2,1:T(8,128)} %get-tuple-element.1090, f32[6,512,4096]{2,1,0:T(8,128)} %fusion.248, f32[6,512]{1,0:T(8,128)S(1)} %dynamic-slice_bitcast_fusion.4, pred[512,4096]{1,0:T(8,128)(4,1)S(1)} %broadcast_compare_fusion.5, pred[]{:T(512)S(6)} %compare.8, ...), kind=kOutput, calls=%fused_computation.49.clone.1 | convolution fusion | flops 1664090112 | bytes 65417220 | tf_op jit(solution)/shard_map/while/body/eval_jaxpr/hqk,qhd->khd/dot_general | solution.py:128
  685.9 37.2 %multiply_reduce_fusion.8 = (f32[6,512]{1,0:T(8,128)S(1)}, f32[6,512,4096]{2,1,0:T(8,128)}) fusion(f32[6,512,4096]{2,1,0:T(8,128)} %fusion.248, f32[6,512]{1,0:T(8,128)S(1)} %dynamic-slice_bitcast_fusion.4, pred[512,4096]{1,0:T(8,128)(4,1)S(1)} %broadcast_compare_fusion.5, bf16[4096,6,64]{0,2,1:T(8,128)(2,1)} %get-tuple-element.1112, ...), kind=kOutput, calls=%fused_computation.44.clone.1 | convolution fusion | flops 1673524224 | bytes 106323968 | tf_op jit(solution)/shard_map/while/body/eval_jaxpr/qhd,khd->hqk/dot_general | solution.py:131
  723.1 41.0 %multiply_convert_fusion.12 = bf16[6,512,4096]{2,1,0:T(8,128)(2,1)} fusion(f32[6,512,4096]{2,1,0:T(8,128)} %get-tuple-element.981, f32[6,512,4096]{2,1,0:T(8,128)} %fusion.248, f32[6,512]{1,0:T(8,128)S(1)} %get-tuple-element.982, f32[6,512]{1,0:T(8,128)S(1)} %dynamic-slice_bitcast_fusion.4, pred[512,4096]{1,0:T(8,128)(4,1)S(1)} %broadcast_compare_fusion.5), kind=kLoop, calls=%fused_computation.43.clone.1 | loop fusion | flops 75497472 | bytes 127950848 | tf_op jit(solution)/shard_map/while/body/eval_jaxpr/convert_element_type | solution.py:135
  829.0 26.3 %reduce-scatter.25.cloned.1.call-done = bf16[512,768]{1,0:T(8,128)(2,1)} async-done(((bf16[1024,768]{1,0:T(8,128)(2,1)}), bf16[512,768]{1,0:T(8,128)(2,1)}) %reduce-scatter.25.cloned.1.call-update) | async-done | bytes 786448 | tf_op jit(solution)/shard_map/reduce_scatter | solution.py:47
  859.8 27.3 %all-gather.24.cloned.1.call-done = bf16[1024,768]{1,0:T(8,128)(2,1)} async-done(((bf16[512,768]{1,0:T(8,128)(2,1)}), bf16[1024,768]{1,0:T(8,128)(2,1)}) %all-gather.24.cloned.1.call-update) | async-done | bytes 1572880 | tf_op jit(solution)/shard_map/all_gather | solution.py:63
  899.3 52.6 %while.58 = (s32[]{:T(128)}, f32[1024,6,64]{0,2,1:T(8,128)S(1)}, f32[1024,6,64]{0,2,1:T(8,128)}, bf16[2,512,6,64]{1,3,2,0:T(8,128)(2,1)}, bf16[2,512,6,64]{1,3,2...) while((s32[]{:T(128)}, f32[1024,6,64]{0,2,1:T(8,128)S(1)}, ...), condition=%wide.region_24.25_spmd.clone, body=%wide.region_22.24_spmd.clone.sunk | while | flops 2064184320 | bytes 132759976 | solution.py:150
  1084.2 40.4 %reduce-scatter.51.cloned.1.call-done = f32[48,1024]{1,0:T(8,128)} async-done(((f32[768,1024]{1,0:T(8,128)}), f32[48,1024]{1,0:T(8,128)}) %reduce-scatter.51.cloned.1.call-update) | async-done | bytes 196624 | tf_op jit(solution)/shard_map/reduce_scatter | solution.py:358
  1141.6 52.0 %reduce-scatter.49.cloned.1.call-done = f32[48,1024]{1,0:T(8,128)} async-done(((f32[768,1024]{1,0:T(8,128)}), f32[48,1024]{1,0:T(8,128)}) %reduce-scatter.49.cloned.1.call-update) | async-done | bytes 196624 | tf_op jit(solution)/shard_map/reduce_scatter | solution.py:357
  1210.7 43.4 %reduce-scatter.47.cloned.1.call-done = f32[48,384]{1,0:T(8,128)} async-done(((f32[768,384]{1,0:T(8,128)}), f32[48,384]{1,0:T(8,128)}) %reduce-scatter.47.cloned.1.call-update) | async-done | bytes 73744 | tf_op jit(solution)/shard_map/reduce_scatter | solution.py:356
  1269.5 45.4 %reduce-scatter.41.cloned.1.call-done = f32[48,384]{1,0:T(8,128)} async-done(((f32[768,384]{1,0:T(8,128)}), f32[48,384]{1,0:T(8,128)}) %reduce-scatter.41.cloned.1.call-update) | async-done | bytes 73744 | tf_op jit(solution)/shard_map/reduce_scatter | solution.py:353
  1330.2 45.3 %reduce-scatter.43.cloned.1.call-done = f32[48,384]{1,0:T(8,128)} async-done(((f32[768,384]{1,0:T(8,128)}), f32[48,384]{1,0:T(8,128)}) %reduce-scatter.43.cloned.1.call-update) | async-done | bytes 73744 | tf_op jit(solution)/shard_map/reduce_scatter | solution.py:354
  1390.9 45.3 %reduce-scatter.45.cloned.1.call-done = f32[48,384]{1,0:T(8,128)} async-done(((f32[768,384]{1,0:T(8,128)}), f32[48,384]{1,0:T(8,128)}) %reduce-scatter.45.cloned.1.call-update) | async-done | bytes 73744 | tf_op jit(solution)/shard_map/reduce_scatter | solution.py:355
  1451.7 45.1 %reduce-scatter.37.cloned.1.call-done = f32[48,384]{1,0:T(8,128)} async-done(((f32[768,384]{1,0:T(8,128)}), f32[48,384]{1,0:T(8,128)}) %reduce-scatter.37.cloned.1.call-update) | async-done | bytes 73744 | tf_op jit(solution)/shard_map/reduce_scatter | solution.py:351
  1512.1 45.2 %reduce-scatter.35.cloned.1.call-done = f32[48,384]{1,0:T(8,128)} async-done(((f32[768,384]{1,0:T(8,128)}), f32[48,384]{1,0:T(8,128)}) %reduce-scatter.35.cloned.1.call-update) | async-done | bytes 73744 | tf_op jit(solution)/shard_map/reduce_scatter | solution.py:350
  1572.7 45.2 %reduce-scatter.33.cloned.1.call-done = f32[48,384]{1,0:T(8,128)} async-done(((f32[768,384]{1,0:T(8,128)}), f32[48,384]{1,0:T(8,128)}) %reduce-scatter.33.cloned.1.call-update) | async-done | bytes 73744 | tf_op jit(solution)/shard_map/reduce_scatter | solution.py:349
  1633.2 45.3 %reduce-scatter.39.cloned.1.call-done = f32[48,384]{1,0:T(8,128)} async-done(((f32[768,384]{1,0:T(8,128)}), f32[48,384]{1,0:T(8,128)}) %reduce-scatter.39.cloned.1.call-update) | async-done | bytes 73744 | tf_op jit(solution)/shard_map/reduce_scatter | solution.py:352
  1694.0 57.6 %all-reduce.9 = (f32[768]{0:T(1024)S(1)}, f32[768]{0:T(1024)S(1)}, f32[768]{0:T(1024)S(1)}) all-reduce(f32[768]{0:T(1024)S(1)} %reshape.482, f32[768]{0:T(1024)S(1)} %reshape.484, f32[768]{0:T(1024)S(1)} %reshape.486), channel_id=9, replica_groups=mesh['dp'=4,'wide'=4,'narrow'=2] {'dp','wide'}, use_global_device_ids=true, to_apply=%region_31.32.clone | all-reduce | flops 2304 | bytes 18432
  (503 shorter events, 764.5 us)
Async XLA Ops:
  8.1 108.7 %reduce-scatter.21.cloned.1.call-start = ((), (), s32[]{:S(2)}) async-start(), calls=%async_computation.18 | async-start | bytes 2359296 | tf_op jit(solution)/shard_map/reduce_scatter | solution.py:47
  89.1 59.9 %all-gather.10.cloned.1.call-start = ((), (), s32[]{:S(2)}) async-start(), calls=%async_computation.19 | async-start | bytes 2359296 | tf_op jit(solution)/shard_map/all_gather | solution.py:59
  121.1 204.9 %reduce-scatter.23.cloned.1.call-start = ((), (), s32[]{:S(2)}) async-start(), calls=%async_computation.20 | async-start | bytes 2359296 | tf_op jit(solution)/shard_map/reduce_scatter | solution.py:47
  299.8 31.3 %all-gather.16.cloned.1.call-start = ((), (), s32[]{:S(2)}) async-start(), calls=%async_computation.23 | async-start | bytes 1966080 | tf_op jit(solution)/shard_map/all_gather | solution.py:205
  300.4 56.5 %all-gather.12.cloned.1.call-start = ((), (), s32[]{:S(2)}) async-start(), calls=%async_computation.21 | async-start | bytes 2359296 | tf_op jit(solution)/shard_map/all_gather | solution.py:59
  300.4 143.5 %copy-start.61 = (f32[768]{0:T(1024)}, f32[768]{0:T(1024)S(1)}, u32[]{:S(2)}) copy-start(f32[768]{0:T(1024)S(1)} %convert_element_type.279) | copy-start | bytes 9220
  327.4 116.5 %copy-start.67 = (f32[512]{0:T(512)}, f32[512]{0:T(512)S(1)}, u32[]{:S(2)}) copy-start(f32[512]{0:T(512)S(1)} %fusion.110) | copy-start | bytes 6148
  329.7 48.1 %all-gather.14.cloned.1.call-start = ((), (), s32[]{:S(2)}) async-start(), calls=%async_computation.22 | async-start | bytes 1966080 | tf_op jit(solution)/shard_map/all_gather | solution.py:204
  330.3 68.7 %all-gather.18.cloned.1.call-start = ((), (), s32[]{:S(2)}) async-start(), calls=%async_computation.24 | async-start | bytes 1966080 | tf_op jit(solution)/shard_map/all_gather | solution.py:206
  331.0 110.0 %reduce-scatter.27.cloned.1.call-start = ((), (), s32[]{:S(2)}) async-start(), calls=%async_computation.27 | async-start | bytes 2359296 | tf_op jit(solution)/shard_map/reduce_scatter | solution.py:53
  414.8 59.0 %all-gather.22.cloned.1.call-start = ((), (), s32[]{:S(2)}) async-start(), calls=%async_computation.28 | async-start | bytes 2359296 | tf_op jit(solution)/shard_map/all_gather | solution.py:63
  446.6 380.1 %reduce-scatter.29.cloned.1.call-start = ((), (), s32[]{:S(2)}) async-start(), calls=%async_computation.29 | async-start | bytes 2359296 | tf_op jit(solution)/shard_map/reduce_scatter | solution.py:53
  800.6 54.8 %reduce-scatter.25.cloned.1.call-start = ((), (), s32[]{:S(2)}) async-start(), calls=%async_computation.25 | async-start | bytes 2359296 | tf_op jit(solution)/shard_map/reduce_scatter | solution.py:47
  805.4 50.0 %copy-start.16 = (bf16[512,768]{1,0:T(8,128)(2,1)S(1)}, bf16[512,768]{1,0:T(8,128)(2,1)}, u32[]{:S(2)}) copy-start(bf16[512,768]{1,0:T(8,128)(2,1)} %reduce-scatter.27.cloned.1.call-done) | copy-start | bytes 2359300
  805.4 50.0 %copy-start.62 = (f32[768]{0:T(1024)S(1)}, f32[768]{0:T(1024)}, u32[]{:S(2)}) copy-start(f32[768]{0:T(1024)} %copy-done.61) | copy-start | bytes 9220
  805.4 81.7 %all-gather.24.cloned.1.call-start = ((), (), s32[]{:S(2)}) async-start(), calls=%async_computation.30 | async-start | bytes 2359296 | tf_op jit(solution)/shard_map/all_gather | solution.py:63
  859.7 179.3 %reduce-scatter.31.cloned.1.call-start = ((), (), s32[]{:S(2)}) async-start(), calls=%async_computation.31 | async-start | bytes 2359296 | tf_op jit(solution)/shard_map/reduce_scatter | solution.py:53
  959.4 108.4 %reduce-scatter.53.cloned.1.call-start = ((), (), s32[]{:S(2)}) async-start(), calls=%async_computation.43 | async-start | bytes 3342336 | tf_op jit(solution)/shard_map/reduce_scatter | solution.py:359
  964.8 159.8 %reduce-scatter.51.cloned.1.call-start = ((), (), s32[]{:S(2)}) async-start(), calls=%async_computation.42 | async-start | bytes 3342336 | tf_op jit(solution)/shard_map/reduce_scatter | solution.py:358
  971.9 221.8 %reduce-scatter.49.cloned.1.call-start = ((), (), s32[]{:S(2)}) async-start(), calls=%async_computation.41 | async-start | bytes 3342336 | tf_op jit(solution)/shard_map/reduce_scatter | solution.py:357
  977.4 276.8 %reduce-scatter.47.cloned.1.call-start = ((), (), s32[]{:S(2)}) async-start(), calls=%async_computation.40 | async-start | bytes 1253376 | tf_op jit(solution)/shard_map/reduce_scatter | solution.py:356
  982.9 332.0 %reduce-scatter.41.cloned.1.call-start = ((), (), s32[]{:S(2)}) async-start(), calls=%async_computation.37 | async-start | bytes 1253376 | tf_op jit(solution)/shard_map/reduce_scatter | solution.py:353
  987.1 388.4 %reduce-scatter.43.cloned.1.call-start = ((), (), s32[]{:S(2)}) async-start(), calls=%async_computation.38 | async-start | bytes 1253376 | tf_op jit(solution)/shard_map/reduce_scatter | solution.py:354
  999.0 437.2 %reduce-scatter.45.cloned.1.call-start = ((), (), s32[]{:S(2)}) async-start(), calls=%async_computation.39 | async-start | bytes 1253376 | tf_op jit(solution)/shard_map/reduce_scatter | solution.py:355
  1014.4 437.3 %all-gather.20.cloned.1.call-start = ((), (), s32[]{:S(2)}) async-start(), calls=%async_computation.26 | async-start | bytes 2359296 | tf_op jit(solution)/shard_map/all_gather | solution.py:59
  1015.0 481.8 %reduce-scatter.37.cloned.1.call-start = ((), (), s32[]{:S(2)}) async-start(), calls=%async_computation.35 | async-start | bytes 1253376 | tf_op jit(solution)/shard_map/reduce_scatter | solution.py:351
  1024.4 533.0 %reduce-scatter.35.cloned.1.call-start = ((), (), s32[]{:S(2)}) async-start(), calls=%async_computation.34 | async-start | bytes 1253376 | tf_op jit(solution)/shard_map/reduce_scatter | solution.py:350
  1028.4 589.5 %reduce-scatter.33.cloned.1.call-start = ((), (), s32[]{:S(2)}) async-start(), calls=%async_computation.33 | async-start | bytes 1253376 | tf_op jit(solution)/shard_map/reduce_scatter | solution.py:349
  1032.2 646.3 %reduce-scatter.39.cloned.1.call-start = ((), (), s32[]{:S(2)}) async-start(), calls=%async_computation.36 | async-start | bytes 1253376 | tf_op jit(solution)/shard_map/reduce_scatter | solution.py:352
  1038.7 731.9 %all-gather.26.cloned.1.call-start = ((), (), s32[]{:S(2)}) async-start(), calls=%async_computation.32 | async-start | bytes 2359296 | tf_op jit(solution)/shard_map/all_gather | solution.py:63
  1044.5 726.1 %reduce-scatter.55.cloned.1.call-start = ((), (), s32[]{:S(2)}) async-start(), calls=%async_computation.44 | async-start | bytes 9437184
  1140.7 310.9 %copy-start.77 = (f32[768]{0:T(1024)S(1)}, f32[768]{0:T(1024)}, u32[]{:S(2)}) copy-start(f32[768]{0:T(1024)} %get-tuple-element.596) | copy-start | bytes 9220
  (88 other events, 910.6 us)
Sparse Core Ops, SparseCore 0:
  89.1 27.2 reduce-scatter.20
  121.2 27.6 all-gather.9
  299.9 26.0 reduce-scatter.22
  414.9 26.0 reduce-scatter.26
  859.9 27.2 all-gather.23
  959.5 26.0 reduce-scatter.30
  989.4 66.1 reduce-scatter.52
  1059.5 65.1 reduce-scatter.50
  1128.4 65.1 reduce-scatter.48
  1197.1 56.9 reduce-scatter.46
  1257.7 57.1 reduce-scatter.40
  1318.4 57.1 reduce-scatter.42
  1379.1 57.0 reduce-scatter.44
  1439.7 57.0 reduce-scatter.36
  1500.3 57.0 reduce-scatter.34
  1560.9 56.9 reduce-scatter.32
  1621.4 57.0 reduce-scatter.38
  1680.6 76.2 reduce-scatter.54
Sparse Core Ops, SparseCore 1:
  301.8 19.5 all-gather.15
  329.8 27.0 all-gather.11
  358.3 19.5 all-gather.13
  379.4 19.5 all-gather.17
  446.7 27.0 all-gather.21
  800.7 25.9 reduce-scatter.28
  829.4 26.0 reduce-scatter.24
  1016.5 27.0 all-gather.19
  1045.6 27.1 all-gather.25
where the time goes:
time: 1800 us; the launch traced here: 1790 us
  waiting for transfers between devices  670 us (37%)
  matrix products  475 us (26%)
  blocking collectives  302 us (17%)
  other arithmetic  214 us (12%)
  local copies, waits for them, and re-layouts  86.7 us (5%)
  between operations  19.6 us (1%)
    convert_element_type x4, other arithmetic, one_block(): score_grad = (probabilities * (prob_grad - centre)).astype(jnp.bfloat16)  95.8 us
    dot_general x8, matrix products, one_block(): jnp.einsum('qhd,khd->hqk', query_part, key_heads, preferred_element_type=...  94.9 us
    dot_general x4, matrix products, one_block(): jnp.einsum('qhd,khd->hqk', grad_part, value_heads, preferred_element_type...  88.5 us
    unnamed x3, blocking collectives  75 us
    dot_general x4, matrix products, one_block(): jnp.einsum('hqk,qhd->khd', low_probabilities, grad_part, preferred_elemen...  55.6 us
    all_gather x3, waiting for transfers between devices, whole_grads(): return lax.all_gather(share, 'narrow', axis=0, tiled=True)  54.4 us
    reduce_sum x4, other arithmetic, one_block(): normalizer = jnp.sum(exponent, axis=2, keepdims=True)  52.3 us
    dot_general x4, matrix products, one_block(): jnp.einsum('hqk,khd->qhd', probabilities, value_heads, preferred_element_...  52.2 us
  transfers between devices with their start and end apart: 27, of which 20 were waited for; matrix products, arithmetic and copies ran while one was open for 9% of the time, Pallas kernels for 0%

commit v1 on v0

v1 whole, which is shorter than its diff:
```python
import functools
import math

import jax
import jax.numpy as jnp
from jax import lax
from jax.experimental import pallas as pl
from jax.experimental.pallas import tpu as pltpu
from jax.sharding import PartitionSpec as P

F32 = jnp.float32
BF16 = jnp.bfloat16
EPSILON = 1e-06
ROOT_TWO_OVER_PI = 0.7978845608028654
CUBIC = 0.044715
HEAD_DIM = 64
PAIR = 2 * HEAD_DIM
SCALE = HEAD_DIM ** (-0.5)
EXP2_SCALE = SCALE * math.log2(math.e)
HIDE = 1e30
TILE = 256

NN = (((1,), (0,)), ((), ()))
NT = (((1,), (1,)), ((), ()))
TN = (((0,), (0,)), ((), ()))


def dot(left, right, dims):
    return lax.dot_general(left, right, dims, preferred_element_type=F32)


def params():
    return pltpu.CompilerParams(vmem_limit_bytes=60 * 1024 * 1024)


def cost(flops, nbytes):
    return pl.CostEstimate(flops=int(flops), bytes_accessed=int(nbytes), transcendentals=0)


def shape_of(shape, dtype):
    return jax.ShapeDtypeStruct(shape, dtype)


def whole(shape):
    zeros = (0,) * len(shape)
    return pl.BlockSpec(shape, lambda *_: zeros)


def rows(width, height=TILE):
    return pl.BlockSpec((height, width), lambda t, *_: (t, 0))


def inverse_rms(values):
    return lax.rsqrt(jnp.mean(values * values, axis=1, keepdims=True) + EPSILON)


def norm_back(values, gain, upstream):
    factor = inverse_rms(values)
    scaled = upstream * gain
    mean = jnp.mean(values * scaled, axis=1, keepdims=True)
    grad = factor * scaled - values * (factor * factor * factor * mean)
    return grad, jnp.sum(upstream * values * factor, axis=0, keepdims=True)


def in_half(shape, half):
    return (lax.broadcasted_iota(jnp.int32, shape, 1) // HEAD_DIM) == half


def only_half(values, half):
    return jnp.where(in_half(values.shape, half), values, jnp.zeros_like(values))


def order_kernel(seg, blk, table, x, gy, xp, gyp, row_ids, col_ids, pos_out, scalars, pos):
    step = pl.program_id(0)
    count = seg.shape[1]

    @pl.when(step == 0)
    def _():
        segments = seg[...]
        image = jnp.zeros_like(segments)
        for s in range(table.shape[1]):
            image = jnp.where(segments == s, table[0, s], image)
        first = (image == 0).astype(F32)
        before = lax.broadcasted_iota(jnp.int32, (count, count), 0) < lax.broadcasted_iota(
            jnp.int32, (count, count), 1
        )
        rank = dot(
            jnp.broadcast_to(first, (8, count)).astype(BF16),
            before.astype(F32).astype(BF16),
            NN,
        )[0:1]
        total = jnp.sum(first)
        index = lax.broadcasted_iota(jnp.int32, (1, count), 1).astype(F32)
        place = jnp.where(image == 0, rank, total + index - rank)
        pos[...] = place.astype(jnp.int32)
        pos_out[...] = jnp.broadcast_to(pos[...], (8, count))
        n0 = total.astype(jnp.int32)
        tiles = count // TILE
        visits0 = jnp.maximum(1, (n0 + TILE - 1) // TILE)
        start1 = jnp.minimum(tiles - 1, n0 // TILE)
        visits = visits0 + tiles - start1
        for v in range(tiles + 1):
            real = jnp.minimum(v, visits - 1)
            in_first = real < visits0
            scalars[v] = jnp.where(in_first, real, real - visits0 + start1)
            scalars[8 + v] = jnp.where(in_first, 0, 1)
        scalars[16] = visits
        scalars[17] = n0

    onehot = (
        lax.broadcasted_iota(jnp.int32, (TILE, count), 0) + step * TILE == pos[...]
    ).astype(F32).astype(BF16)
    xp[...] = dot(onehot, x[...], NN).astype(BF16)
    gyp[...] = dot(onehot, gy[...], NN).astype(BF16)
    ids = jnp.concatenate(
        [
            seg[...].astype(F32),
            blk[...].astype(F32),
            jnp.zeros((126, count), F32),
        ],
        axis=0,
    ).astype(BF16)
    row_ids[...] = dot(ids[0:8], onehot, NT)
    col_ids[...] = dot(onehot, ids, NT)


def order_rows(seg, blk, table, x, gy):
    count, width = x.shape
    return pl.pallas_call(
        order_kernel,
        grid=(count // TILE,),
        in_specs=[
            whole((1, count)),
            whole((1, count)),
            pl.BlockSpec(memory_space=pltpu.SMEM),
            whole((count, width)),
            whole((count, width)),
        ],
        out_specs=[
            rows(width),
            rows(width),
            pl.BlockSpec((8, TILE), lambda t: (0, t)),
            rows(128),
            whole((8, count)),
            pl.BlockSpec(memory_space=pltpu.SMEM),
        ],
        out_shape=[
            shape_of((count, width), BF16),
            shape_of((count, width), BF16),
            shape_of((8, count), F32),
            shape_of((count, 128), F32),
            shape_of((8, count), jnp.int32),
            shape_of((32,), jnp.int32),
        ],
        scratch_shapes=[pltpu.VMEM((1, count), jnp.int32)],
        compiler_params=params(),
        cost_estimate=cost(4 * count * count * width, 8 * count * width),
    )(seg, blk, table, x, gy)


def restore_kernel(pos, values, out):
    count = values.shape[0]
    onehot = (
        lax.broadcasted_iota(jnp.int32, (count, TILE), 0) == pos[0:1, :]
    ).astype(F32).astype(BF16)
    out[...] = dot(onehot, values[...], TN).astype(BF16)


def restore_rows(pos, values):
    count, width = values.shape
    return pl.pallas_call(
        restore_kernel,
        grid=(count // TILE,),
        in_specs=[pl.BlockSpec((8, TILE), lambda t: (0, t)), whole((count, width))],
        out_specs=rows(width),
        out_shape=shape_of((count, width), BF16),
        compiler_params=params(),
        cost_estimate=cost(2 * count * count * width, 4 * count * width),
    )(pos, values)


def project_kernel(x, gain, weight, normed, out):
    values = x[...].astype(F32)
    n1 = (values * inverse_rms(values) * gain[...]).astype(BF16)
    normed[...] = n1
    out[...] = dot(n1, weight[...], NN).astype(BF16)


def norm_project(x, gain, weight):
    count, width = x.shape
    outs = weight.shape[1]
    return pl.pallas_call(
        project_kernel,
        grid=(count // TILE,),
        in_specs=[rows(width), whole((1, width)), whole(weight.shape)],
        out_specs=[rows(width), rows(outs)],
        out_shape=[shape_of((count, width), BF16), shape_of((count, outs), BF16)],
        compiler_params=params(),
        cost_estimate=cost(2 * count * width * outs, 4 * count * width + 2 * count * outs),
    )(x, gain, weight)


SELF_TILE = 128
SELF_WINDOW = 512
BACK_WINDOW = 640


def store_logs(ref, columns, logs, extra=None):
    spread = jnp.where(in_half((logs[0].shape[0], PAIR), 0), logs[0], logs[1]).T
    for half in range(2):
        line = spread[half * HEAD_DIM : half * HEAD_DIM + 1, :]
        if extra is not None:
            line = jnp.where(extra, line, ref[half : half + 1, columns])
        ref[half : half + 1, columns] = line


def self_forward_kernel(q, k, v, row_ids, col_ids, out, logs):
    count = q.shape[0]
    for tile in range(count // SELF_TILE):
        base = tile * SELF_TILE
        start = min(max(base - 256, 0), count - SELF_WINDOW)
        spot = slice(base, base + SELF_TILE)
        window = slice(start, start + SELF_WINDOW)
        seen = (col_ids[spot, 0:1] == row_ids[0:1, window]) & (
            row_ids[1:2, window] <= col_ids[spot, 1:2]
        )
        bias = jnp.where(seen, 0.0, -HIDE)
        keys = k[window, :]
        values = v[window, :]
        queries = q[spot, :]
        parts, totals = [], []
        for half in range(2):
            scores = dot(only_half(queries, half), keys, NT) * EXP2_SCALE + bias
            highest = jnp.max(scores, axis=1, keepdims=True)
            weights = jnp.exp2(scores - highest)
            total = jnp.sum(weights, axis=1, keepdims=True)
            parts.append(dot(weights.astype(BF16), values, NN) / total)
            totals.append(highest + jnp.log2(total))
        out[spot, :] = jnp.where(in_half(parts[0].shape, 0), parts[0], parts[1]).astype(BF16)
        store_logs(logs, spot, totals)


def self_forward(qkv, row_ids, col_ids):
    count = qkv.shape[0]
    inner = qkv.shape[1] // 3
    pairs = inner // PAIR

    def part(which):
        return pl.BlockSpec((count, PAIR), lambda p: (0, which * pairs + p))

    return pl.pallas_call(
        self_forward_kernel,
        grid=(pairs,),
        in_specs=[part(0), part(1), part(2), whole((8, count)), whole((count, 128))],
        out_specs=[
            pl.BlockSpec((count, PAIR), lambda p: (0, p)),
            pl.BlockSpec((8, count), lambda p: (p, 0)),
        ],
        out_shape=[shape_of((count, inner), BF16), shape_of((8 * pairs, count), F32)],
        compiler_params=params(),
        cost_estimate=cost(16 * count * SELF_WINDOW * inner, 8 * count * inner),
    )(qkv, qkv, qkv, row_ids, col_ids)


def self_backward_kernel(q, k, v, grad, logs, deltas, row_ids, col_ids, dq, dk, dv, key_sum, value_sum):
    count = q.shape[0]
    key_sum[...] = jnp.zeros_like(key_sum)
    value_sum[...] = jnp.zeros_like(value_sum)
    for tile in range(count // TILE):
        base = tile * TILE
        start = min(max(base - 256, 0), count - BACK_WINDOW)
        spot = slice(base, base + TILE)
        window = slice(start, start + BACK_WINDOW)
        seen = (col_ids[window, 0:1] == row_ids[0:1, spot]) & (
            col_ids[window, 1:2] <= row_ids[1:2, spot]
        )
        bias = jnp.where(seen, 0.0, -HIDE)
        keys = k[window, :]
        values = v[window, :]
        queries = q[spot, :]
        grads = grad[spot, :]
        parts = []
        for half in range(2):
            one_query = only_half(queries, half)
            one_grad = only_half(grads, half)
            scores = dot(keys, one_query, NT) * EXP2_SCALE + bias
            weights = jnp.exp2(scores - logs[half : half + 1, spot])
            slopes = dot(values, one_grad, NT)
            pushed = (weights * (slopes - deltas[half : half + 1, spot])).astype(BF16)
            value_sum[window, :] += dot(weights.astype(BF16), one_grad, NN)
            key_sum[window, :] += dot(pushed, one_query, NN)
            parts.append(dot(pushed, keys, TN))
        dq[spot, :] = (
            jnp.where(in_half(parts[0].shape, 0), parts[0], parts[1]) * SCALE
        ).astype(BF16)
    dk[...] = (key_sum[...] * SCALE).astype(BF16)
    dv[...] = value_sum[...].astype(BF16)


def self_backward(qkv, grad, logs, deltas, row_ids, col_ids):
    count = qkv.shape[0]
    inner = qkv.shape[1] // 3
    pairs = inner // PAIR

    def part(which):
        return pl.BlockSpec((count, PAIR), lambda p: (0, which * pairs + p))

    line = pl.BlockSpec((8, count), lambda p: (p, 0))
    return pl.pallas_call(
        self_backward_kernel,
        grid=(pairs,),
        in_specs=[
            part(0),
            part(1),
            part(2),
            part(0),
            line,
            line,
            whole((8, count)),
            whole((count, 128)),
        ],
        out_specs=[part(0)] * 3,
        out_shape=[shape_of((count, inner), BF16)] * 3,
        scratch_shapes=[pltpu.VMEM((count, PAIR), F32)] * 2,
        compiler_params=params(),
        cost_estimate=cost(40 * count * BACK_WINDOW * inner, 16 * count * inner),
    )(qkv, qkv, qkv, grad, logs, deltas, row_ids, col_ids)


def cross_forward_kernel(scalars, q, k, v, out, logs):
    step = pl.program_id(1)
    tile = scalars[step]
    image = scalars[8 + step]
    again = (step > 0) & (scalars[jnp.maximum(step - 1, 0)] == tile)

    @pl.when(step < scalars[16])
    def _():
        queries = q[...]
        keys = k[...]
        values = v[...]
        parts, totals = [], []
        for half in range(2):
            scores = dot(only_half(queries, half), keys, NT)
            highest = jnp.max(scores, axis=1, keepdims=True) * EXP2_SCALE
            weights = jnp.exp2(scores * EXP2_SCALE - highest)
            total = jnp.sum(weights, axis=1, keepdims=True)
            parts.append(dot(weights.astype(BF16), values, NN) / total)
            totals.append(highest + jnp.log2(total))
        mixed = jnp.where(in_half(parts[0].shape, 0), parts[0], parts[1]).astype(BF16)
        limit = scalars[17] - tile * TILE
        row_mine = (
            lax.broadcasted_iota(jnp.int32, mixed.shape, 0) >= limit
        ) == (image == 1)
        lane_mine = (
            lax.broadcasted_iota(jnp.int32, (1, TILE), 1) >= limit
        ) == (image == 1)
        keep = jnp.logical_not(again)
        out[...] = jnp.where(row_mine | keep, mixed, out[...])
        store_logs(logs, slice(0, TILE), totals, lane_mine | keep)


def cross_forward(scalars, q, keys_values, images):
    count, inner = q.shape
    pairs = inner // PAIR
    memory_rows = keys_values.shape[0] // images
    tile_spec = pl.BlockSpec((TILE, PAIR), lambda p, s, sc: (sc[s], p))

    def part(which):
        return pl.BlockSpec(
            (memory_rows, PAIR), lambda p, s, sc: (sc[8 + s], which * pairs + p)
        )

    return pl.pallas_call(
        cross_forward_kernel,
        grid_spec=pltpu.PrefetchScalarGridSpec(
            num_scalar_prefetch=1,
            grid=(pairs, count // TILE + 1),
            in_specs=[tile_spec, part(0), part(1)],
            out_specs=[
                tile_spec,
                pl.BlockSpec((8, TILE), lambda p, s, sc: (p, sc[s])),
            ],
        ),
        out_shape=[shape_of((count, inner), BF16), shape_of((8 * pairs, count), F32)],
        compiler_params=params(),
        cost_estimate=cost(20 * count * memory_rows * inner, 8 * memory_rows * inner),
    )(scalars, q, keys_values, keys_values)


def cross_backward_kernel(
    scalars, q, k, v, grad, logs, deltas, dq, dk, dv, key_sum, value_sum
):
    step = pl.program_id(1)
    tile = scalars[step]
    image = scalars[8 + step]
    before = jnp.maximum(step - 1, 0)
    visits = scalars[16]
    again = (step > 0) & (scalars[before] == tile)
    first = (step == 0) | (scalars[8 + before] != image)
    after = jnp.minimum(step + 1, visits - 1)
    last = (step == visits - 1) | (scalars[8 + after] != image)

    @pl.when(first)
    def _():
        key_sum[...] = jnp.zeros_like(key_sum)
        value_sum[...] = jnp.zeros_like(value_sum)

    @pl.when(step < visits)
    def _():
        queries = q[...]
        grads = grad[...]
        keys = k[...]
        values = v[...]
        limit = scalars[17] - tile * TILE
        lane_mine = (
            lax.broadcasted_iota(jnp.int32, (1, TILE), 1) >= limit
        ) == (image == 1)
        parts = []
        for half in range(2):
            one_query = only_half(queries, half)
            one_grad = only_half(grads, half)
            log = jnp.where(lane_mine, logs[half : half + 1, :], HIDE)
            scores = dot(keys, one_query, NT)
            weights = jnp.exp2(scores * EXP2_SCALE - log)
            slopes = dot(values, one_grad, NT)
            pushed = (weights * (slopes - deltas[half : half + 1, :])).astype(BF16)
            value_sum[...] += dot(weights.astype(BF16), one_grad, NN)
            key_sum[...] += dot(pushed, one_query, NN)
            parts.append(dot(pushed, keys, TN))
        grad_query = (
            jnp.where(in_half(parts[0].shape, 0), parts[0], parts[1]) * SCALE
        ).astype(BF16)
        dq[...] = jnp.where(again, dq[...] + grad_query, grad_query)

        @pl.when(last)
        def _():
            dk[...] = (key_sum[...] * SCALE).astype(BF16)
            dv[...] = value_sum[...].astype(BF16)


def cross_backward(scalars, q, keys_values, grad, logs, deltas, images):
    count, inner = q.shape
    pairs = inner // PAIR
    memory_rows = keys_values.shape[0] // images
    tile_spec = pl.BlockSpec((TILE, PAIR), lambda p, s, sc: (sc[s], p))
    line = pl.BlockSpec((8, TILE), lambda p, s, sc: (p, sc[s]))

    def part(which):
        return pl.BlockSpec(
            (memory_rows, PAIR), lambda p, s, sc: (sc[8 + s], which * pairs + p)
        )

    return pl.pallas_call(
        cross_backward_kernel,
        grid_spec=pltpu.PrefetchScalarGridSpec(
            num_scalar_prefetch=1,
            grid=(pairs, count // TILE + 1),
            in_specs=[tile_spec, part(0), part(1), tile_spec, line, line],
            out_specs=[tile_spec, part(0), part(0)],
            scratch_shapes=[pltpu.VMEM((memory_rows, PAIR), F32)] * 2,
        ),
        out_shape=[
            shape_of((count, inner), BF16),
            shape_of((images * memory_rows, inner), BF16),
            shape_of((images * memory_rows, inner), BF16),
        ],
        compiler_params=params(),
        cost_estimate=cost(50 * count * memory_rows * inner, 16 * memory_rows * inner),
    )(scalars, q, keys_values, keys_values, grad, logs, deltas)


def middle_kernel(x, mine, theirs, out_mine, out_theirs, gain, query, h1, n2, cq):
    values = (
        x[...].astype(F32)
        + dot(mine[...], out_mine[...], NT)
        + dot(theirs[...], out_theirs[...], NT)
    )
    h1[...] = values
    normed = (values * inverse_rms(values) * gain[...]).astype(BF16)
    n2[...] = normed
    cq[...] = dot(normed, query[...], NN).astype(BF16)


def middle_step(x, mine, theirs, out_mine, out_theirs, gain, query):
    count, width = x.shape
    half = mine.shape[1]
    return pl.pallas_call(
        middle_kernel,
        grid=(count // TILE,),
        in_specs=[
            rows(width),
            rows(half),
            rows(half),
            whole(out_mine.shape),
            whole(out_theirs.shape),
            whole((1, width)),
            whole(query.shape),
        ],
        out_specs=[rows(width), rows(width), rows(half)],
        out_shape=[
            shape_of((count, width), F32),
            shape_of((count, width), BF16),
            shape_of((count, half), BF16),
        ],
        compiler_params=params(),
        cost_estimate=cost(6 * count * width * half, 12 * count * width),
    )(x, mine, theirs, out_mine, out_theirs, gain, query)


def head_sums(left, right):
    product = left.astype(F32) * right.astype(F32)
    width = product.shape[1]
    high = product.astype(BF16)
    low = (product - high.astype(F32)).astype(BF16)
    height = 8 * (width // PAIR)
    line = lax.broadcasted_iota(jnp.int32, (height, width), 0)
    head = lax.broadcasted_iota(jnp.int32, (height, width), 1) // HEAD_DIM
    choose = (
        ((line // 8) * 2 + line % 8 == head) & (line % 8 < 2)
    ).astype(F32).astype(BF16)
    return dot(choose, high, NT) + dot(choose, low, NT)


def units_kernel(
    h1,
    mine,
    theirs,
    out_mine,
    out_theirs,
    gain,
    gy,
    gate_mine,
    up_mine,
    down_mine,
    gate_theirs,
    up_theirs,
    down_theirs,
    output,
    n3,
    hidden,
    grad_gate,
    grad_up,
    dh2,
    e2,
    dc,
    deltas,
    gain_grad,
):
    values = (
        h1[...] + dot(mine[...], out_mine[...], NT) + dot(theirs[...], out_theirs[...], NT)
    )
    normed = (values * inverse_rms(values) * gain[...]).astype(BF16)
    n3[...] = normed
    upstream = gy[...]
    mixed = jnp.zeros_like(values)
    back = jnp.zeros_like(values)
    for own in (True, False):
        gate_weight = gate_mine if own else gate_theirs
        up_weight = up_mine if own else up_theirs
        down_weight = down_mine if own else down_theirs
        gate = dot(normed, gate_weight[...], NN)
        up = dot(normed, up_weight[...], NN)
        square = gate * gate
        bend = jnp.tanh(ROOT_TWO_OVER_PI * gate * (1.0 + CUBIC * square))
        lift = 0.5 * (1.0 + bend)
        gelu = gate * lift
        slope = lift + (0.5 * ROOT_TWO_OVER_PI) * gate * (1.0 - bend * bend) * (
            1.0 + (3.0 * CUBIC) * square
        )
        units = (gelu * up).astype(BF16)
        mixed = mixed + dot(units, down_weight[...], NT)
        pushed = dot(upstream, down_weight[...], NN)
        push_gate = (pushed * up * slope).astype(BF16)
        push_up = (pushed * gelu).astype(BF16)
        back = (
            back + dot(push_gate, gate_weight[...], NT) + dot(push_up, up_weight[...], NT)
        )
        if own:
            hidden[...] = units
            grad_gate[...] = push_gate
            grad_up[...] = push_up
    output[...] = (values + mixed).astype(BF16)
    grad, gain_part = norm_back(values, gain[...], back)
    result = upstream.astype(F32) + grad
    dh2[...] = result
    low = result.astype(BF16)
    e2[...] = low
    crossed = dot(low, out_mine[...], NN).astype(BF16)
    dc[...] = crossed
    deltas[...] = head_sums(crossed, mine[...])

    @pl.when(pl.program_id(0) == 0)
    def _():
        gain_grad[...] = jnp.zeros_like(gain_grad)

    gain_grad[0:1, :] += gain_part


def units_step(h1, mine, theirs, out_mine, out_theirs, gain, gy, own, other):
    count, width = h1.shape
    half = mine.shape[1]
    unit = own[0].shape[1]
    lines = 8 * (half // PAIR)
    return pl.pallas_call(
        units_kernel,
        grid=(count // TILE,),
        in_specs=[
            rows(width),
            rows(half),
            rows(half),
            whole(out_mine.shape),
            whole(out_theirs.shape),
            whole((1, width)),
            rows(width),
        ]
        + [whole((width, unit))] * 6,
        out_specs=[
            rows(width),
            rows(width),
            rows(unit),
            rows(unit),
            rows(unit),
            rows(width),
            rows(width),
            rows(half),
            pl.BlockSpec((lines, TILE), lambda t: (0, t)),
            whole((8, width)),
        ],
        out_shape=[
            shape_of((count, width), BF16),
            shape_of((count, width), BF16),
            shape_of((count, unit), BF16),
            shape_of((count, unit), BF16),
            shape_of((count, unit), BF16),
            shape_of((count, width), F32),
            shape_of((count, width), BF16),
            shape_of((count, half), BF16),
            shape_of((lines, count), F32),
            shape_of((8, width), F32),
        ],
        compiler_params=params(),
        cost_estimate=cost(30 * count * width * unit, 30 * count * width),
    )(h1, mine, theirs, out_mine, out_theirs, gain, gy, *own, *other)


def turn_kernel(
    dh2, h1, mine, theirs, query_mine, query_theirs, gain, out_mine, attended,
    dh1, e1, da, deltas, gain_grad,
):
    back = dot(mine[...], query_mine[...], NT) + dot(theirs[...], query_theirs[...], NT)
    grad, gain_part = norm_back(h1[...], gain[...], back)
    result = dh2[...] + grad
    dh1[...] = result
    low = result.astype(BF16)
    e1[...] = low
    pushed = dot(low, out_mine[...], NN).astype(BF16)
    da[...] = pushed
    deltas[...] = head_sums(pushed, attended[...])

    @pl.when(pl.program_id(0) == 0)
    def _():
        gain_grad[...] = jnp.zeros_like(gain_grad)

    gain_grad[0:1, :] += gain_part


def turn_step(dh2, h1, mine, theirs, query_mine, query_theirs, gain, out_mine, attended):
    count, width = h1.shape
    half = mine.shape[1]
    lines = 8 * (half // PAIR)
    return pl.pallas_call(
        turn_kernel,
        grid=(count // TILE,),
        in_specs=[
            rows(width),
            rows(width),
            rows(half),
            rows(half),
            whole(query_mine.shape),
            whole(query_theirs.shape),
            whole((1, width)),
            whole(out_mine.shape),
            rows(half),
        ],
        out_specs=[
            rows(width),
            rows(width),
            rows(half),
            pl.BlockSpec((lines, TILE), lambda t: (0, t)),
            whole((8, width)),
        ],
        out_shape=[
            shape_of((count, width), F32),
            shape_of((count, width), BF16),
            shape_of((count, half), BF16),
            shape_of((lines, count), F32),
            shape_of((8, width), F32),
        ],
        compiler_params=params(),
        cost_estimate=cost(6 * count * width * half, 16 * count * width),
    )(dh2, h1, mine, theirs, query_mine, query_theirs, gain, out_mine, attended)


def partial_kernel(dq, dk, dv, weight, out):
    inner = dq.shape[1]
    out[...] = (
        dot(dq[...], weight[:, 0:inner], NT)
        + dot(dk[...], weight[:, inner : 2 * inner], NT)
        + dot(dv[...], weight[:, 2 * inner : 3 * inner], NT)
    ).astype(BF16)


def partial_step(dq, dk, dv, weight):
    count, inner = dq.shape
    width = weight.shape[0]
    return pl.pallas_call(
        partial_kernel,
        grid=(count // TILE,),
        in_specs=[rows(inner)] * 3 + [whole(weight.shape)],
        out_specs=rows(width),
        out_shape=shape_of((count, width), BF16),
        compiler_params=params(),
        cost_estimate=cost(6 * count * width * inner, 8 * count * width),
    )(dq, dk, dv, weight)


def first_kernel(dh1, x, mine, theirs, gain, out, gain_grad):
    back = mine[...].astype(F32) + theirs[...].astype(F32)
    grad, gain_part = norm_back(x[...].astype(F32), gain[...], back)
    out[...] = (dh1[...] + grad).astype(BF16)

    @pl.when(pl.program_id(0) == 0)
    def _():
        gain_grad[...] = jnp.zeros_like(gain_grad)

    gain_grad[0:1, :] += gain_part


def first_step(dh1, x, mine, theirs, gain):
    count, width = x.shape
    return pl.pallas_call(
        first_kernel,
        grid=(count // TILE,),
        in_specs=[rows(width)] * 4 + [whole((1, width))],
        out_specs=[rows(width), whole((8, width))],
        out_shape=[shape_of((count, width), BF16), shape_of((8, width), F32)],
        compiler_params=params(),
        cost_estimate=cost(20 * count * width, 12 * count * width),
    )(dh1, x, mine, theirs, gain)


def swap(values, axis, distance):
    size = lax.axis_size(axis)
    return lax.ppermute(values, axis, [(i, i ^ distance) for i in range(size)])


def gather_wide(piece):
    other = swap(piece, "wide", 2)
    pair = jnp.stack([piece, other])
    return pair, swap(pair, "wide", 1)


def in_order(mine, theirs):
    index = lax.axis_index("wide")
    core, chip = index % 2, index // 2
    even = jnp.where(core == 0, mine, theirs)
    odd = jnp.where(core == 0, theirs, mine)
    first = jnp.where(chip == 0, 0, 1)
    parts = []
    for c in range(2):
        for source in (even, odd):
            parts.append(jnp.where(first == c, source[0], source[1]))
    return jnp.concatenate(parts, axis=0)


def sum_line(values):
    size = lax.axis_size("dp")
    if size != 4:
        return lax.psum(values, "dp")
    place = lax.axis_index("dp")
    inner = (place == 1) | (place == 2)
    got = lax.ppermute(values, "dp", [(0, 1), (3, 2)])
    part = jnp.where(inner, values + got, values)
    got = lax.ppermute(part, "dp", [(1, 2), (2, 1)])
    total = part + got
    got = lax.ppermute(total, "dp", [(1, 0), (2, 3)])
    return jnp.where(inner, total, got)


def sum_gradient(gradient):
    height, width = gradient.shape
    index = lax.axis_index("wide")
    core, chip = index % 2, index // 2
    split = gradient.astype(BF16).reshape(2, 2, height // 4, width)
    keep = lax.dynamic_index_in_dim(split, core, 1, False)
    send = lax.dynamic_index_in_dim(split, 1 - core, 1, False)
    part = (keep.astype(F32) + swap(send, "wide", 1).astype(F32)).astype(BF16)
    keep = lax.dynamic_index_in_dim(part, chip, 0, False)
    send = lax.dynamic_index_in_dim(part, 1 - chip, 0, False)
    part = (keep.astype(F32) + swap(send, "wide", 2).astype(F32)).astype(BF16)
    return sum_line(part)


def contract_rows(left, right):
    return dot(left, right, TN)


def local(
    tokens,
    memory,
    cotangent,
    norm1_gain,
    norm2_gain,
    norm3_gain,
    q_weight,
    k_weight,
    v_weight,
    o_weight,
    cross_q,
    cross_k,
    cross_v,
    cross_o,
    gate_weight,
    up_weight,
    down_weight,
    segment_ids,
    block_ids,
    image_table,
):
    width = tokens.shape[1]
    share = q_weight.shape[0]
    inner = q_weight.shape[1]
    unit = gate_weight.shape[1]
    images = memory.shape[0]
    flat_memory = memory.reshape(-1, width)

    gains = jnp.stack([norm1_gain, norm2_gain, norm3_gain])
    gains = jnp.pad(gains, ((0, 13), (0, 3 * inner - share)))
    early = jnp.concatenate(
        [jnp.concatenate([q_weight, k_weight, v_weight], axis=1), gains], axis=0
    )
    early = in_order(*gather_wide(early)).reshape(4, share + 16, 3 * inner)
    qkv_weight = early[:, :share].reshape(4 * share, 3 * inner)
    all_gains = (
        jnp.swapaxes(early[:, share : share + 3, :share], 0, 1)
        .reshape(3, 1, 4 * share)
        .astype(F32)
    )
    mid = jnp.concatenate([o_weight, cross_o, cross_q, cross_k, cross_v], axis=1)
    mid_mine, mid_core = gather_wide(mid)
    mid_full = in_order(mid_mine, mid_core)
    out_mine = mid_full[:, 0:inner]
    cross_out_mine = mid_full[:, inner : 2 * inner]
    cross_query_mine = mid_full[:, 2 * inner : 3 * inner]
    cross_kv = mid_full[:, 3 * inner : 5 * inner]
    mid_y = swap(mid_mine[:, :, : 3 * inner], "narrow", 1)
    mid_other = in_order(mid_y, swap(mid_y, "wide", 1))
    out_theirs = mid_other[:, 0:inner]
    cross_out_theirs = mid_other[:, inner : 2 * inner]
    cross_query_theirs = mid_other[:, 2 * inner : 3 * inner]
    late = jnp.concatenate([gate_weight, up_weight, down_weight], axis=1)
    late_mine, late_core = gather_wide(late)
    late_full = in_order(late_mine, late_core)
    late_y = swap(late_mine, "narrow", 1)
    late_other = in_order(late_y, swap(late_y, "wide", 1))
    units_mine = [late_full[:, i * unit : (i + 1) * unit] for i in range(3)]
    units_theirs = [late_other[:, i * unit : (i + 1) * unit] for i in range(3)]

    x, gy, row_ids, col_ids, pos, scalars = order_rows(
        segment_ids, block_ids, image_table, tokens, cotangent
    )
    n1, qkv = norm_project(x, all_gains[0], qkv_weight)
    attended, self_logs = self_forward(qkv, row_ids, col_ids)
    attended_theirs = swap(attended, "narrow", 1)
    keys_values = dot(flat_memory, cross_kv, NN).astype(BF16)
    h1, n2, cq = middle_step(
        x, attended, attended_theirs, out_mine, out_theirs, all_gains[1], cross_query_mine
    )
    crossed, cross_logs = cross_forward(scalars, cq, keys_values, images)
    crossed_theirs = swap(crossed, "narrow", 1)
    (
        output,
        n3,
        hidden,
        grad_gate,
        grad_up,
        dh2,
        e2,
        dc,
        cross_deltas,
        third_gain,
    ) = units_step(
        h1,
        crossed,
        crossed_theirs,
        cross_out_mine,
        cross_out_theirs,
        all_gains[2],
        gy,
        units_mine,
        units_theirs,
    )

    unit_grads = sum_gradient(
        jnp.concatenate(
            [
                contract_rows(n3, grad_gate).astype(BF16),
                contract_rows(n3, grad_up).astype(BF16),
                contract_rows(gy, hidden).astype(BF16),
            ],
            axis=1,
        )
    )
    dcq, dck, dcv = cross_backward(
        scalars, cq, keys_values, dc, cross_logs, cross_deltas, images
    )
    dcq_theirs = swap(dcq, "narrow", 1)
    memory_part = (
        dot(dck, cross_kv[:, :inner], NT) + dot(dcv, cross_kv[:, inner:], NT)
    ).astype(BF16)
    side = lax.axis_index("narrow")
    memory_keep = lax.dynamic_slice_in_dim(memory_part, side * inner, inner, 1)
    memory_send = lax.dynamic_slice_in_dim(memory_part, (1 - side) * inner, inner, 1)
    memory_grad = (
        memory_keep.astype(F32) + swap(memory_send, "narrow", 1).astype(F32)
    ).astype(BF16)
    memory_grad = memory_grad.reshape(images, -1, inner)
    cross_grads = sum_gradient(
        jnp.concatenate(
            [
                contract_rows(n2, dcq).astype(BF16),
                contract_rows(flat_memory, dck).astype(BF16),
                contract_rows(flat_memory, dcv).astype(BF16),
                contract_rows(e2, crossed).astype(BF16),
            ],
            axis=1,
        )
    )
    dh1, e1, da, self_deltas, second_gain = turn_step(
        dh2,
        h1,
        dcq,
        dcq_theirs,
        cross_query_mine,
        cross_query_theirs,
        all_gains[1],
        out_mine,
        attended,
    )
    dq, dk, dv = self_backward(qkv, da, self_logs, self_deltas, row_ids, col_ids)
    dn1 = partial_step(dq, dk, dv, qkv_weight)
    dn1_theirs = swap(dn1, "narrow", 1)
    tokens_grad, first_gain = first_step(dh1, x, dn1, dn1_theirs, all_gains[0])
    tokens_grad = restore_rows(pos, tokens_grad)
    output = restore_rows(pos, output)
    self_grads = sum_gradient(
        jnp.concatenate(
            [
                contract_rows(n1, dq).astype(BF16),
                contract_rows(n1, dk).astype(BF16),
                contract_rows(n1, dv).astype(BF16),
                contract_rows(e1, attended).astype(BF16),
            ],
            axis=1,
        )
    )
    gain_lines = jnp.concatenate(
        [first_gain[0:1], second_gain[0:1], third_gain[0:1]], axis=0
    )
    gain_sums = lax.psum(gain_lines, ("dp", "wide"))
    gain_sums = lax.dynamic_slice_in_dim(
        gain_sums, lax.axis_index("wide") * share, share, 1
    )

    def grads(array, size, count):
        return [array[:, i * size : (i + 1) * size].astype(F32) for i in range(count)]

    gate_grad, up_grad, down_grad = grads(unit_grads, unit, 3)
    cross_q_grad, cross_k_grad, cross_v_grad, cross_o_grad = grads(cross_grads, inner, 4)
    q_grad, k_grad, v_grad, o_grad = grads(self_grads, inner, 4)
    return (
        output,
        tokens_grad,
        memory_grad,
        gain_sums[0],
        gain_sums[1],
        gain_sums[2],
        q_grad,
        k_grad,
        v_grad,
        o_grad,
        cross_q_grad,
        cross_k_grad,
        cross_v_grad,
        cross_o_grad,
        gate_grad,
        up_grad,
        down_grad,
    )


def solution(mesh):
    both = ("dp", "wide")
    weight = P("wide", "narrow")
    in_specs = (
        (P(both, None), P(both, None, None), P(both, None))
        + (P("wide"),) * 3
        + (weight,) * 11
        + (P(both, None),) * 3
    )
    out_specs = (
        (P(both, None), P(both, None), P(both, None, "narrow"))
        + (P("wide"),) * 3
        + (weight,) * 11
    )
    return jax.shard_map(local, mesh=mesh, in_specs=in_specs, out_specs=out_specs, check_vma=False)
```

time: 1800 us -> 619 us (0.34)
  the two profiles are of different devices: /device:TPU:0 before, /device:TPU:2 now
where the time goes in v1:
time: 619 us; the launch traced here: 608 us
  Pallas kernels  204 us (33%)
  waiting for transfers between devices  172 us (28%)
  blocking collectives  66 us (11%)
  matrix products  50.3 us (8%)
  other arithmetic  46.7 us (8%)
  local copies, waits for them, and re-layouts  37.1 us (6%)
  starting transfers between devices  30.2 us (5%)
    ppermute x21, waiting for transfers between devices, swap(): return lax.ppermute(values, axis, [(i, i ^ distance) for i in range(size)])  97.7 us
    ppermute x3, waiting for transfers between devices, sum_line(): got = lax.ppermute(total, 'dp', [(1, 0), (2, 3)])  70.7 us
    psum x1, blocking collectives, local(): gain_sums = lax.psum(gain_lines, ('dp', 'wide'))  66 us
    pallas_call x1, Pallas kernels, cross_backward(): pl.pallas_call(cross_backward_kernel, grid_spec=pltpu.PrefetchScalarGridS...  51.1 us
    dot_general x14, matrix products, dot(): return lax.dot_general(left, right, dims, preferred_element_type=F32)  50.3 us
    pallas_call x1, Pallas kernels, units_step(): pl.pallas_call(units_kernel, grid=(count // TILE,), in_specs=[rows(width)...  36.4 us
    pallas_call x1, Pallas kernels, cross_forward(): pl.pallas_call(cross_forward_kernel, grid_spec=pltpu.PrefetchScalarGridSp...  33 us
    pallas_call x1, Pallas kernels, self_forward(): pl.pallas_call(self_forward_kernel, grid=(pairs,), in_specs=[part(0), par...  15.4 us
  transfers between devices with their start and end apart: 30, of which 10 were waited for; matrix products, arithmetic and copies ran while one was open for 18% of the time, Pallas kernels for 19%

profile of v1, /device:TPU:2, one launch (start us, length us, event | category | flops | bytes accessed | tf_op | source)
XLA Modules:
  0.0 607.7 jit_solution(15955197674429418076)
XLA Ops:
  8.4 9.5 %collective-permute-done = bf16[208,1152]{1,0:T(8,128)(2,1)S(1)} collective-permute-done((bf16[208,1152]{1,0:T(8,128)(2,1)S(1)}, bf16[208,1152]{1,0:T(8,128)(2,1)S(1)}, u32[]{:S(2)}, u32[]{:S(2)}) %collective-permute-start) | collective-permute-done | bytes 479264 | tf_op jit(solution)/shard_map/ppermute | solution.py:754
  19.7 8.0 %shard_map.323 = (bf16[1024,768]{1,0:T(8,128)(2,1)}, bf16[1024,768]{1,0:T(8,128)(2,1)}, f32[8,1024]{1,0:T(8,128)}, f32[1024,128]{1,0:T(8,128)}, s32[8,1024]{1,0:T(8,128)}, /*index=5*/s32[32]{0:T(128)}) custom-call(s32[1,1024]{1,0:T(1,128)} %seg.1, s32[1,1024]{1,0:T(1,128)} %blk.1, s32[1,8]{1,0:T(1,128)} %table.1, bf16[1024,768]{1,0:T(8,128)(2,1)} %x.3, ...), custom_call_target="tpu_custom_call" | custom-call | flops 3221225472 | bytes 6291456 | tf_op jit(solution)/shard_map/pallas_call | solution.py:129
  27.8 5.9 collective-permute-done.3
  37.5 20.4 %collective-permute-done.8 = bf16[192,3072]{1,0:T(8,128)(2,1)} collective-permute-done((bf16[192,3072]{1,0:T(8,128)(2,1)S(1)}, bf16[192,3072]{1,0:T(8,128)(2,1)}, u32[]{:S(2)}, u32[]{:S(2)}) %collective-permute-start.8) | collective-permute-done | bytes 1179680 | tf_op jit(solution)/shard_map/ppermute | solution.py:754
  66.2 6.1 %shard_map.324 = (bf16[1024,768]{1,0:T(8,128)(2,1)}, bf16[1024,1152]{1,0:T(8,128)(2,1)}) custom-call(bf16[1024,768]{1,0:T(8,128)(2,1)} %get-tuple-element.56.x, f32[1,768]{1,0:T(1,128)} %squeeze.36.gain, bf16[768,1152]{1,0:T(8,128)(2,1)} %bitcast.150), custom_call_target="tpu_custom_call" | custom-call | flops 1811939328 | bytes 5505024 | tf_op jit(solution)/shard_map/pallas_call | solution.py:192
  72.4 15.4 %shard_map.325 = (bf16[1024,384]{1,0:T(8,128)(2,1)}, f32[24,1024]{1,0:T(8,128)}) custom-call(bf16[1024,1152]{1,0:T(8,128)(2,1)} %get-tuple-element.57.q.k.v, bf16[1024,1152]{1,0:T(8,128)(2,1)} %get-tuple-element.57.q.k.v, bf16[1024,1152]{1,0:T(8,128)(2,1)} %get-tuple-element.57.q.k.v, f32[8,1024]{1,0:T(8,128)} %get-tuple-element.58.row_ids, ...), custom_call_target="tpu_custom_call" | custom-call | flops 3221225472 | bytes 3145728 | tf_op jit(solution)/shard_map/pallas_call | solution.py:251
  91.7 4.5 pad_maximum_fusion.3
  96.3 7.4 %fusion.k.v = bf16[4096,768]{1,0:T(8,128)(2,1)} fusion(bf16[4096,768]{1,0:T(8,128)(2,1)S(1)} %bitcast.128, bf16[768,1920]{1,0:T(8,128)(2,1)S(1)} %pad_maximum_fusion.3), kind=kOutput, calls=%fused_computation.3 | convolution fusion | flops 4834983936 | bytes 13762560 | tf_op jit(solution)/shard_map/dot_general | solution.py:29
  108.0 23.7 %collective-permute-done.2.theirs = bf16[1024,384]{1,0:T(8,128)(2,1)} collective-permute-done((bf16[1024,384]{1,0:T(8,128)(2,1)}, bf16[1024,384]{1,0:T(8,128)(2,1)}, u32[]{:S(2)}, u32[]{:S(2)}) %collective-permute-start.2) | collective-permute-done | bytes 786464 | tf_op jit(solution)/shard_map/ppermute | solution.py:754
  131.7 7.6 %shard_map.326 = (f32[1024,768]{1,0:T(8,128)}, bf16[1024,768]{1,0:T(8,128)(2,1)}, bf16[1024,384]{1,0:T(8,128)(2,1)}) custom-call(bf16[1024,768]{1,0:T(8,128)(2,1)} %get-tuple-element.56.x, bf16[1024,384]{1,0:T(8,128)(2,1)} %get-tuple-element.60.mine.attended, bf16[1024,384]{1,0:T(8,128)(2,1)} %collective-permute-done.2.theirs, ...), custom_call_target="tpu_custom_call" | custom-call | flops 1811939328 | bytes 9437184 | tf_op jit(solution)/shard_map/pallas_call | solution.py:487
  139.3 33.0 %shard_map.327 = (bf16[1024,384]{1,0:T(8,128)(2,1)}, f32[24,1024]{1,0:T(8,128)}) custom-call(s32[32]{0:T(128)} %get-tuple-element.62.scalars, bf16[1024,384]{1,0:T(8,128)(2,1)} %get-tuple-element.63.q, bf16[4096,768]{1,0:T(8,128)(2,1)} %fusion.k.v, bf16[4096,768]{1,0:T(8,128)(2,1)} %fusion.k.v), custom_call_target="tpu_custom_call" | custom-call | flops 16106127360 | bytes 6291456 | tf_op jit(solution)/shard_map/pallas_call | solution.py:373
  184.3 7.5 %collective-permute-done.7.theirs = bf16[1024,384]{1,0:T(8,128)(2,1)} collective-permute-done((bf16[1024,384]{1,0:T(8,128)(2,1)}, bf16[1024,384]{1,0:T(8,128)(2,1)}, u32[]{:S(2)}, u32[]{:S(2)}) %collective-permute-start.7) | collective-permute-done | bytes 786464 | tf_op jit(solution)/shard_map/ppermute | solution.py:754
  191.9 36.4 %shard_map.328 = (bf16[1024,768]{1,0:T(8,128)(2,1)}, bf16[1024,768]{1,0:T(8,128)(2,1)}, bf16[1024,1024]{1,0:T(8,128)(2,1)}, bf16[1024,1024]{1,0:T(8,128)(2,1)}, ...) custom-call(f32[1024,768]{1,0:T(8,128)} %get-tuple-element.61.h1, ...), custom_call_target="tpu_custom_call" | custom-call | flops 24159191040 | bytes 23592960 | tf_op jit(solution)/shard_map/pallas_call | solution.py:604
  228.3 51.1 %shard_map.330 = (bf16[1024,384]{1,0:T(8,128)(2,1)}, bf16[4096,384]{1,0:T(8,128)(2,1)}, bf16[4096,384]{1,0:T(8,128)(2,1)}) custom-call(s32[32]{0:T(128)} %get-tuple-element.62.scalars, bf16[1024,384]{1,0:T(8,128)(2,1)} %get-tuple-element.63.q, bf16[4096,768]{1,0:T(8,128)(2,1)} %fusion.k.v, bf16[4096,768]{1,0:T(8,128)(2,1)} %fusion.k.v, ...), custom_call_target="tpu_custom_call" | custom-call | flops 40265318400 | bytes 12582912 | tf_op jit(solution)/shard_map/pallas_call | solution.py:453
  279.5 5.6 fusion.11
  285.0 6.4 %fusion.6 = bf16[768,384]{0,1:T(8,128)(2,1)} fusion(bf16[4096,384]{1,0:T(8,128)(2,1)S(1)} %copy-done.2, bf16[4096,768]{1,0:T(8,128)(2,1)} %bitcast.124), kind=kOutput, calls=%fused_computation.44 | convolution fusion | flops 2416214016 | bytes 10027008 | tf_op jit(solution)/shard_map/dot_general | solution.py:29
  293.0 6.3 %fusion.5 = bf16[768,384]{0,1:T(8,128)(2,1)} fusion(bf16[4096,384]{1,0:T(8,128)(2,1)S(1)} %copy-done.1, bf16[4096,768]{1,0:T(8,128)(2,1)} %bitcast.125), kind=kOutput, calls=%fused_computation.43 | convolution fusion | flops 2416214016 | bytes 10027008 | tf_op jit(solution)/shard_map/dot_general | solution.py:29
  299.2 5.7 add_convert_fusion
  330.5 4.9 shard_map.329
  335.4 10.2 %shard_map.331 = (f32[1024,768]{1,0:T(8,128)}, bf16[1024,768]{1,0:T(8,128)(2,1)}, bf16[1024,384]{1,0:T(8,128)(2,1)}, f32[24,1024]{1,0:T(8,128)}, f32[8,768]{1,0:T(8,128)}) custom-call(f32[1024,768]{1,0:T(8,128)} %get-tuple-element.67.dh2, f32[1024,768]{1,0:T(8,128)} %get-tuple-element.61.h1, bf16[1024,384]{1,0:T(8,128)(2,1)} %get-tuple-element.71.mine, ...), custom_call_target="tpu_custom_call" | custom-call | flops 1811939328 | bytes 12582912 | tf_op jit(solution)/shard_map/pallas_call | solution.py:671
  345.6 13.9 %shard_map.332 = (bf16[1024,384]{1,0:T(8,128)(2,1)}, bf16[1024,384]{1,0:T(8,128)(2,1)}, bf16[1024,384]{1,0:T(8,128)(2,1)}) custom-call(bf16[1024,1152]{1,0:T(8,128)(2,1)} %get-tuple-element.57.q.k.v, bf16[1024,1152]{1,0:T(8,128)(2,1)} %get-tuple-element.57.q.k.v, bf16[1024,1152]{1,0:T(8,128)(2,1)} %get-tuple-element.57.q.k.v, ...), custom_call_target="tpu_custom_call" | custom-call | flops 10066329600 | bytes 6291456 | tf_op jit(solution)/shard_map/pallas_call | solution.py:309
  364.6 6.3 %shard_map.333.mine = bf16[1024,768]{1,0:T(8,128)(2,1)} custom-call(bf16[1024,384]{1,0:T(8,128)(2,1)} %get-tuple-element.76.dq, bf16[1024,384]{1,0:T(8,128)(2,1)} %get-tuple-element.77.dk, bf16[1024,384]{1,0:T(8,128)(2,1)} %get-tuple-element.78.dv, bf16[768,1152]{1,0:T(8,128)(2,1)} %bitcast.151), custom_call_target="tpu_custom_call" | custom-call | flops 1811939328 | bytes 6291456 | tf_op jit(solution)/shard_map/pallas_call | solution.py:716
  378.5 4.3 copy.46
  391.6 10.7 %collective-permute-done.21 = bf16[192,1536]{1,0:T(8,128)(2,1)S(1)} collective-permute-done((bf16[192,1536]{1,0:T(8,128)(2,1)S(1)}, bf16[192,1536]{1,0:T(8,128)(2,1)S(1)}, u32[]{:S(2)}, u32[]{:S(2)}) %collective-permute-start.21) | collective-permute-done | bytes 589856 | tf_op jit(solution)/shard_map/ppermute | solution.py:754
  407.7 19.9 %collective-permute-done.26 = bf16[192,3072]{1,0:T(8,128)(2,1)S(1)} collective-permute-done((bf16[192,3072]{1,0:T(8,128)(2,1)S(1)}, bf16[192,3072]{1,0:T(8,128)(2,1)S(1)}, u32[]{:S(2)}, u32[]{:S(2)}) %collective-permute-start.26) | collective-permute-done | bytes 1179680 | tf_op jit(solution)/shard_map/ppermute | solution.py:754
  429.1 4.5 collective-permute-start.27
  433.7 5.8 shard_map.334
  441.7 66.0 %psum.7 = f32[3,768]{1,0:T(4,128)S(1)} all-reduce(f32[3,768]{1,0:T(4,128)S(1)} %pad_maximum_fusion.12), channel_id=1, replica_groups=mesh['dp'=4,'wide'=4,'narrow'=2] {'dp','wide'}, use_global_device_ids=true, to_apply=%region_0.1 | all-reduce | flops 2304 | bytes 18432 | tf_op jit(solution)/shard_map/psum | solution.py:970
  507.7 5.1 shard_map.335
  525.5 4.4 add_convert_fusion.1
  534.2 47.5 %collective-permute-done.19 = bf16[192,1536]{1,0:T(8,128)(2,1)S(1)} collective-permute-done((bf16[192,1536]{1,0:T(8,128)(2,1)S(1)}, bf16[192,1536]{1,0:T(8,128)(2,1)S(1)}, u32[]{:S(2)}, u32[]{:S(2)}) %collective-permute-start.19) | collective-permute-done | bytes 589856 | tf_op jit(solution)/shard_map/ppermute | solution.py:786
  582.8 23.2 %collective-permute-done.29 = bf16[192,3072]{1,0:T(8,128)(2,1)S(1)} collective-permute-done((bf16[192,3072]{1,0:T(8,128)(2,1)S(1)}, bf16[192,3072]{1,0:T(8,128)(2,1)S(1)}, u32[]{:S(2)}, u32[]{:S(2)}) %collective-permute-start.29) | collective-permute-done | bytes 1179680 | tf_op jit(solution)/shard_map/ppermute | solution.py:786
  (203 shorter events, 118.7 us)
Async XLA Ops:
  4.0 13.9 %collective-permute-start = (bf16[208,1152]{1,0:T(8,128)(2,1)S(1)}, bf16[208,1152]{1,0:T(8,128)(2,1)S(1)}, u32[]{:S(2)}, u32[]{:S(2)}) collective-permute-start(bf16[208,1152]{1,0:T(8,128)(2,1)S(1)} %get-tuple-element.147), channel_id=1, source_target_pairs={{0,4},{2,6},{4,0},{6,2},{1,5},{3,7},{5,1},{7,3},{8,12},{10,14},{12... | collective-permute-start | bytes 1437704 | tf_op jit(solution)/shard_map/ppermute | solution.py:754
  6.1 27.6 %collective-permute-start.3 = (bf16[192,1920]{1,0:T(8,128)(2,1)S(1)}, bf16[192,1920]{1,0:T(8,128)(2,1)S(1)}, u32[]{:S(2)}, u32[]{:S(2)}) collective-permute-start(bf16[192,1920]{1,0:T(8,128)(2,1)S(1)} %constant_dynamic-update-slice_fusion), channel_id=1, source_target_pairs={{0,4},{2,6},{4,0},{6,2},{1,5},{3,7},{5,1},{7,3},{8,12},{10,14},{12... | collective-permute-start | bytes 2211848 | tf_op jit(solution)/shard_map/ppermute | solution.py:754
  8.3 49.7 %collective-permute-start.8 = (bf16[192,3072]{1,0:T(8,128)(2,1)S(1)}, bf16[192,3072]{1,0:T(8,128)(2,1)}, u32[]{:S(2)}, u32[]{:S(2)}) collective-permute-start(bf16[192,3072]{1,0:T(8,128)(2,1)S(1)} %constant_dynamic-update-slice_fusion.5), channel_id=1, source_target_pairs={{0,4},{2,6},{4,0},{6,2},{1,5},{3,7},{5,1},{7,3},{8,12},{10,14},{12... | collective-permute-start | bytes 3538952 | tf_op jit(solution)/shard_map/ppermute | solution.py:754
  19.7 42.7 %collective-permute-start.1 = (bf16[2,208,1152]{2,1,0:T(8,128)(2,1)}, bf16[2,208,1152]{2,1,0:T(8,128)(2,1)}, u32[]{:S(2)}, u32[]{:S(2)}) collective-permute-start(bf16[2,208,1152]{2,1,0:T(8,128)(2,1)} %pad_maximum_fusion.10), channel_id=1, source_target_pairs={{0,2},{2,0},{4,6},{6,4},{1,3},{3,1},{5,7},{7,5},{8,10},{10,8},{12,... | collective-permute-start | bytes 2875400 | tf_op jit(solution)/shard_map/ppermute | solution.py:754
  35.0 54.6 %collective-permute-start.4 = (bf16[2,192,1920]{2,1,0:T(8,128)(2,1)}, bf16[2,192,1920]{2,1,0:T(8,128)(2,1)}, u32[]{:S(2)}, u32[]{:S(2)}) collective-permute-start(bf16[2,192,1920]{2,1,0:T(8,128)(2,1)} %pad_maximum_fusion.9), channel_id=1, source_target_pairs={{0,2},{2,0},{4,6},{6,4},{1,3},{3,1},{5,7},{7,5},{8,10},{10,8},{12,... | collective-permute-start | bytes 4423688 | tf_op jit(solution)/shard_map/ppermute | solution.py:754
  36.0 53.6 %collective-permute-start.5 = (bf16[2,192,1152]{2,1,0:T(8,128)(2,1)}, bf16[2,192,1152]{2,1,0:T(8,128)(2,1)}, u32[]{:S(2)}, u32[]{:S(2)}) collective-permute-start(bf16[2,192,1152]{2,1,0:T(8,128)(2,1)} %fusion.10), channel_id=1, source_target_pairs={{0,1},{1,0},{2,3},{3,2},{4,5},{5,4},{6,7},{7,6},{8,9},{9,8},{10,11... | collective-permute-start | bytes 2654216 | tf_op jit(solution)/shard_map/ppermute | solution.py:754
  60.9 113.0 %collective-permute-start.9 = (bf16[2,192,3072]{2,1,0:T(8,128)(2,1)}, bf16[2,192,3072]{2,1,0:T(8,128)(2,1)}, u32[]{:S(2)}, u32[]{:S(2)}) collective-permute-start(bf16[2,192,3072]{2,1,0:T(8,128)(2,1)} %pad_maximum_fusion.4), channel_id=1, source_target_pairs={{0,2},{2,0},{4,6},{6,4},{1,3},{3,1},{5,7},{7,5},{8,10},{10,8},{12,... | collective-permute-start | bytes 7077896 | tf_op jit(solution)/shard_map/ppermute | solution.py:754
  60.9 113.0 %collective-permute-start.10 = (bf16[2,192,3072]{2,1,0:T(8,128)(2,1)}, bf16[2,192,3072]{2,1,0:T(8,128)(2,1)}, u32[]{:S(2)}, u32[]{:S(2)}) collective-permute-start(bf16[2,192,3072]{2,1,0:T(8,128)(2,1)} %pad_maximum_fusion.4), channel_id=1, source_target_pairs={{0,1},{1,0},{2,3},{3,2},{4,5},{5,4},{6,7},{7,6},{8,9},{9,8},{10,11... | collective-permute-start | bytes 7077896 | tf_op jit(solution)/shard_map/ppermute | solution.py:754
  87.8 44.0 %collective-permute-start.2 = (bf16[1024,384]{1,0:T(8,128)(2,1)}, bf16[1024,384]{1,0:T(8,128)(2,1)}, u32[]{:S(2)}, u32[]{:S(2)}) collective-permute-start(bf16[1024,384]{1,0:T(8,128)(2,1)} %get-tuple-element.60.mine.attended), channel_id=1, source_target_pairs={{0,1},{1,0},{2,3},{3,2},{4,5},{5,4},{6,7},{7,6},{8,9},{9,8},{10,11... | collective-permute-start | bytes 2359304 | tf_op jit(solution)/shard_map/ppermute | solution.py:754
  89.6 15.4 %collective-permute-start.6 = (bf16[2,192,1152]{2,1,0:T(8,128)(2,1)}, bf16[2,192,1152]{2,1,0:T(8,128)(2,1)S(1)}, u32[]{:S(2)}, u32[]{:S(2)}) collective-permute-start(bf16[2,192,1152]{2,1,0:T(8,128)(2,1)} %collective-permute-done.5), channel_id=1, source_target_pairs={{0,2},{2,0},{4,6},{6,4},{1,3},{3,1},{5,7},{7,5},{8,10},{10,8},{12,... | collective-permute-start | bytes 2654216 | tf_op jit(solution)/shard_map/ppermute | solution.py:754
  96.3 183.2 %copy-start.4 = (bf16[768,1920]{1,0:T(8,128)(2,1)}, bf16[768,1920]{1,0:T(8,128)(2,1)S(1)}, u32[]{:S(2)}) copy-start(bf16[768,1920]{1,0:T(8,128)(2,1)S(1)} %pad_maximum_fusion.3) | copy-start | bytes 8847364
  172.4 19.5 %collective-permute-start.7 = (bf16[1024,384]{1,0:T(8,128)(2,1)}, bf16[1024,384]{1,0:T(8,128)(2,1)}, u32[]{:S(2)}, u32[]{:S(2)}) collective-permute-start(bf16[1024,384]{1,0:T(8,128)(2,1)} %get-tuple-element.64.mine), channel_id=1, source_target_pairs={{0,1},{1,0},{2,3},{3,2},{4,5},{5,4},{6,7},{7,6},{8,9},{9,8},{10,11... | collective-permute-start | bytes 2359304 | tf_op jit(solution)/shard_map/ppermute | solution.py:754
  173.9 5.5 collective-permute-start.11
  291.4 44.0 %collective-permute-start.12 = (bf16[1024,384]{1,0:T(8,128)(2,1)}, bf16[1024,384]{1,0:T(8,128)(2,1)}, u32[]{:S(2)}, u32[]{:S(2)}) collective-permute-start(bf16[1024,384]{1,0:T(8,128)(2,1)} %get-tuple-element.71.mine), channel_id=1, source_target_pairs={{0,1},{1,0},{2,3},{3,2},{4,5},{5,4},{6,7},{7,6},{8,9},{9,8},{10,11... | collective-permute-start | bytes 2359304 | tf_op jit(solution)/shard_map/ppermute | solution.py:754
  308.9 216.6 %collective-permute-start.14 = (bf16[4096,384]{1,0:T(8,128)(2,1)}, bf16[4096,384]{1,0:T(8,128)(2,1)}, u32[]{:S(2)}, u32[]{:S(2)}) collective-permute-start(bf16[4096,384]{1,0:T(8,128)(2,1)} %constant_dynamic-slice_fusion.1), channel_id=1, source_target_pairs={{0,1},{1,0},{2,3},{3,2},{4,5},{5,4},{6,7},{7,6},{8,9},{9,8},{10,11... | collective-permute-start | bytes 9437192 | tf_op jit(solution)/shard_map/ppermute | solution.py:754
  318.6 65.8 %collective-permute-start.20 = (bf16[2,192,1536]{2,1,0:T(8,128)(2,1)S(1)}, bf16[2,192,1536]{2,1,0:T(8,128)(2,1)}, u32[]{:S(2)}, u32[]{:S(2)}) collective-permute-start(bf16[2,192,1536]{2,1,0:T(8,128)(2,1)S(1)} %dynamic-slice_bitcast_fusion.2), channel_id=1, source_target_pairs={{0,2},{2,0},{4,6},{6,4},{1,3},{3,1},{5,7},{7,5},{8,10},{10,8},{12,... | collective-permute-start | bytes 3538952 | tf_op jit(solution)/shard_map/ppermute | solution.py:754
  330.5 56.2 %collective-permute-start.25 = (bf16[2,192,3072]{2,1,0:T(8,128)(2,1)}, bf16[2,192,3072]{2,1,0:T(8,128)(2,1)}, u32[]{:S(2)}, u32[]{:S(2)}) collective-permute-start(bf16[2,192,3072]{2,1,0:T(8,128)(2,1)} %dynamic-slice_bitcast_fusion), channel_id=1, source_target_pairs={{0,2},{2,0},{4,6},{6,4},{1,3},{3,1},{5,7},{7,5},{8,10},{10,8},{12,... | collective-permute-start | bytes 7077896 | tf_op jit(solution)/shard_map/ppermute | solution.py:754
  370.9 62.8 %collective-permute-start.13 = (bf16[1024,768]{1,0:T(8,128)(2,1)}, bf16[1024,768]{1,0:T(8,128)(2,1)}, u32[]{:S(2)}, u32[]{:S(2)}) collective-permute-start(bf16[1024,768]{1,0:T(8,128)(2,1)} %shard_map.333.mine), channel_id=1, source_target_pairs={{0,1},{1,0},{2,3},{3,2},{4,5},{5,4},{6,7},{7,6},{8,9},{9,8},{10,11... | collective-permute-start | bytes 4718600 | tf_op jit(solution)/shard_map/ppermute | solution.py:754
  384.2 21.8 %collective-permute-start.15 = (bf16[2,192,1536]{2,1,0:T(8,128)(2,1)S(1)}, bf16[2,192,1536]{2,1,0:T(8,128)(2,1)S(1)}, u32[]{:S(2)}, u32[]{:S(2)}) collective-permute-start(bf16[2,192,1536]{2,1,0:T(8,128)(2,1)S(1)} %dynamic-slice_bitcast_fusion.3), channel_id=1, source_target_pairs={{0,2},{2,0},{4,6},{6,4},{1,3},{3,1},{5,7},{7,5},{8,10},{10,8},{12,... | collective-permute-start | bytes 3538952 | tf_op jit(solution)/shard_map/ppermute | solution.py:754
  386.1 16.2 %collective-permute-start.21 = (bf16[192,1536]{1,0:T(8,128)(2,1)S(1)}, bf16[192,1536]{1,0:T(8,128)(2,1)S(1)}, u32[]{:S(2)}, u32[]{:S(2)}) collective-permute-start(bf16[192,1536]{1,0:T(8,128)(2,1)S(1)} %dynamic-slice_bitcast_fusion.4), channel_id=1, source_target_pairs={{0,4},{2,6},{4,0},{6,2},{1,5},{3,7},{5,1},{7,3},{8,12},{10,14},{12... | collective-permute-start | bytes 1769480 | tf_op jit(solution)/shard_map/ppermute | solution.py:754
  390.1 37.5 %collective-permute-start.26 = (bf16[192,3072]{1,0:T(8,128)(2,1)S(1)}, bf16[192,3072]{1,0:T(8,128)(2,1)S(1)}, u32[]{:S(2)}, u32[]{:S(2)}) collective-permute-start(bf16[192,3072]{1,0:T(8,128)(2,1)S(1)} %dynamic-slice_bitcast_fusion.1), channel_id=1, source_target_pairs={{0,4},{2,6},{4,0},{6,2},{1,5},{3,7},{5,1},{7,3},{8,12},{10,14},{12... | collective-permute-start | bytes 3538952 | tf_op jit(solution)/shard_map/ppermute | solution.py:754
  402.4 31.2 %collective-permute-start.22 = (bf16[192,1536]{1,0:T(8,128)(2,1)S(1)}, bf16[192,1536]{1,0:T(8,128)(2,1)S(1)}, u32[]{:S(2)}, u32[]{:S(2)}) collective-permute-start(bf16[192,1536]{1,0:T(8,128)(2,1)S(1)} %fusion.8), channel_id=1, source_target_pairs={{0,8},{24,16},{1,9},{25,17},{2,10},{26,18},{3,11},{27,19},{4,12},{... | collective-permute-start | bytes 1769480 | tf_op jit(solution)/shard_map/ppermute | solution.py:782
  407.2 106.3 %collective-permute-start.16 = (bf16[192,1536]{1,0:T(8,128)(2,1)}, bf16[192,1536]{1,0:T(8,128)(2,1)}, u32[]{:S(2)}, u32[]{:S(2)}) collective-permute-start(bf16[192,1536]{1,0:T(8,128)(2,1)} %dynamic-slice_bitcast_fusion.5), channel_id=1, source_target_pairs={{0,4},{2,6},{4,0},{6,2},{1,5},{3,7},{5,1},{7,3},{8,12},{10,14},{12... | collective-permute-start | bytes 1769480 | tf_op jit(solution)/shard_map/ppermute | solution.py:754
  429.1 89.7 %collective-permute-start.27 = (bf16[192,3072]{1,0:T(8,128)(2,1)}, bf16[192,3072]{1,0:T(8,128)(2,1)}, u32[]{:S(2)}, u32[]{:S(2)}) collective-permute-start(bf16[192,3072]{1,0:T(8,128)(2,1)} %fusion.2), channel_id=1, source_target_pairs={{0,8},{24,16},{1,9},{25,17},{2,10},{26,18},{3,11},{27,19},{4,12},{... | collective-permute-start | bytes 3538952 | tf_op jit(solution)/shard_map/ppermute | solution.py:782
  440.2 76.0 %collective-permute-start.23 = (bf16[192,1536]{1,0:T(8,128)(2,1)S(1)}, bf16[192,1536]{1,0:T(8,128)(2,1)}, u32[]{:S(2)}, u32[]{:S(2)}) collective-permute-start(bf16[192,1536]{1,0:T(8,128)(2,1)S(1)} %add_select_fusion.1), channel_id=1, source_target_pairs={{8,16},{16,8},{9,17},{17,9},{10,18},{18,10},{11,19},{19,11},{12,20... | collective-permute-start | bytes 1769480 | tf_op jit(solution)/shard_map/ppermute | solution.py:784
  507.7 17.8 %slice-start.2 = ((s8[6291456]{0:T(1024)(128)(4,1)}), s8[2097152]{0:T(1024)(128)(4,1)S(1)}, s32[]{:S(2)}) async-start(s8[6291456]{0:T(1024)(128)(4,1)} %bitcast.129), calls=%async_computation.2 | async-start | bytes 4194304
  514.8 9.9 %collective-permute-start.17 = (bf16[192,1536]{1,0:T(8,128)(2,1)S(1)}, bf16[192,1536]{1,0:T(8,128)(2,1)S(1)}, u32[]{:S(2)}, u32[]{:S(2)}) collective-permute-start(bf16[192,1536]{1,0:T(8,128)(2,1)S(1)} %fusion.9), channel_id=1, source_target_pairs={{0,8},{24,16},{1,9},{25,17},{2,10},{26,18},{3,11},{27,19},{4,12},{... | collective-permute-start | bytes 1769480 | tf_op jit(solution)/shard_map/ppermute | solution.py:782
  517.5 15.6 %collective-permute-start.24 = (bf16[192,1536]{1,0:T(8,128)(2,1)S(1)}, bf16[192,1536]{1,0:T(8,128)(2,1)S(1)}, u32[]{:S(2)}, u32[]{:S(2)}) collective-permute-start(bf16[192,1536]{1,0:T(8,128)(2,1)S(1)} %add.110), channel_id=1, source_target_pairs={{8,0},{16,24},{9,1},{17,25},{10,2},{18,26},{11,3},{19,27},{12,4},{... | collective-permute-start | bytes 1769480 | tf_op jit(solution)/shard_map/ppermute | solution.py:786
  520.5 10.8 %collective-permute-start.28 = (bf16[192,3072]{1,0:T(8,128)(2,1)S(1)}, bf16[192,3072]{1,0:T(8,128)(2,1)S(1)}, u32[]{:S(2)}, u32[]{:S(2)}) collective-permute-start(bf16[192,3072]{1,0:T(8,128)(2,1)S(1)} %add_select_fusion), channel_id=1, source_target_pairs={{8,16},{16,8},{9,17},{17,9},{10,18},{18,10},{11,19},{19,11},{12,20... | collective-permute-start | bytes 3538952 | tf_op jit(solution)/shard_map/ppermute | solution.py:784
  524.8 5.1 collective-permute-start.18
  530.0 51.6 %collective-permute-start.19 = (bf16[192,1536]{1,0:T(8,128)(2,1)S(1)}, bf16[192,1536]{1,0:T(8,128)(2,1)S(1)}, u32[]{:S(2)}, u32[]{:S(2)}) collective-permute-start(bf16[192,1536]{1,0:T(8,128)(2,1)S(1)} %add.106), channel_id=1, source_target_pairs={{8,0},{16,24},{9,1},{17,25},{10,2},{18,26},{11,3},{19,27},{12,4},{... | collective-permute-start | bytes 1769480 | tf_op jit(solution)/shard_map/ppermute | solution.py:786
  531.8 74.2 %collective-permute-start.29 = (bf16[192,3072]{1,0:T(8,128)(2,1)S(1)}, bf16[192,3072]{1,0:T(8,128)(2,1)S(1)}, u32[]{:S(2)}, u32[]{:S(2)}) collective-permute-start(bf16[192,3072]{1,0:T(8,128)(2,1)S(1)} %add.114), channel_id=1, source_target_pairs={{8,0},{16,24},{9,1},{17,25},{10,2},{18,26},{11,3},{19,27},{12,4},{... | collective-permute-start | bytes 3538952 | tf_op jit(solution)/shard_map/ppermute | solution.py:786
  (31 other events, 142.8 us)
